TPU v7x, 32 devices: a whole 2x2x4 slice. The times are simulated.
32 devices in a mesh: section: 2 (over x), batch: 16 (over z, y, core).
Axes of the slice: x: 2, y: 2, z: 4, core: 2. Of those that a mesh axis runs over, the one named last changes fastest.
Arguments:
- tokens: bfloat16 [256, 357, 256], P('batch'), may hold values from -6 to 6
- cotangent: bfloat16 [256, 357, 256], P('batch'), may hold values from -6 to 6
- frame_ids: int32 [256, 357], P('batch'), may hold values from 0 to 21, as said below
- attend_gain: float32 [2, 256], P('section'), may hold values from 0.1 to 1.9
- attend_shift: float32 [2, 256], P('section'), may hold values from -4 to 4
- inward_weight: bfloat16 [2, 256, 768], P('section'), may hold values from -0.375 to 0.375
- inward_bias: float32 [2, 512], P('section'), may hold values from -4 to 4
- outward_weight: bfloat16 [2, 256, 256], P('section'), may hold values from -1.5 to 1.5
- outward_bias: float32 [2, 256], P('section'), may hold values from -4 to 4
- mixing_gain: float32 [2, 256], P('section'), may hold values from 0.1 to 1.9
- mixing_shift: float32 [2, 256], P('section'), may hold values from -4 to 4
- up_weight: bfloat16 [2, 256, 1024], P('section'), may hold values from -0.375 to 0.375
- up_bias: float32 [2, 1024], P('section'), may hold values from -4 to 4
- down_weight: bfloat16 [2, 1024, 256], P('section'), may hold values from -0.1875 to 0.1875
- down_bias: float32 [2, 256], P('section'), may hold values from -4 to 4
Outputs:
- layer_out: bfloat16 [256, 357, 256], P('batch', None, 'section')
- input_grad: float32 [256, 357, 256], P('batch', None, 'section')
- attend_gain_grad: float32 [2, 256], P('section')
- attend_shift_grad: float32 [2, 256], P('section')
- inward_weight_grad: float32 [2, 256, 768], P('section')
- inward_bias_grad: float32 [2, 512], P('section')
- outward_weight_grad: float32 [2, 256, 256], P('section')
- outward_bias_grad: float32 [2, 256], P('section')
- mixing_gain_grad: float32 [2, 256], P('section')
- mixing_shift_grad: float32 [2, 256], P('section')
- up_weight_grad: float32 [2, 256, 1024], P('section')
- up_bias_grad: float32 [2, 1024], P('section')
- down_weight_grad: float32 [2, 1024, 256], P('section')
- down_bias_grad: float32 [2, 256], P('section')
Inputs may be any that keep to these rules, and one draw needn't show every extreme that they name: `frame_ids`: in each sequence the frame ids start at 0 and rise by one every 17 tokens; the first frame holds 1 to 17 tokens, every later frame 17 tokens except that the last may be cut short.
All inputs are finite; a program needn't handle non-finite values.
Results may differ from a plain program's by a relative error of at most 0.014.
Values may be sent and summed in bfloat16 or wider, within the bound.
No kernel may reach another device: no remote copies, remote signals or barrier semaphores. Data moves between devices by JAX's collectives and lax.ppermute only.
A program may use at most 320 MiB of HBM per device.

v0:
```python
import jax
import jax.numpy as jnp
from jax import lax
from jax.sharding import PartitionSpec as P

HEADS = 4
MICRO = 4


epsilon = 1e-05
masked_value = -1e30


def from_behind(block, axis, distance):
    devices = range(lax.axis_size(axis))
    route = [(i - distance, i) for i in devices if i - distance in devices]
    return lax.ppermute(block, axis, route)


def shifted(block, axis, distance):
    devices = range(lax.axis_size(axis))
    route = [((i - distance) % len(devices), i) for i in devices]
    return lax.ppermute(block, axis, route)


def normalize(value, gain, shift):
    center = value - jnp.mean(value, axis=-1, keepdims=True)
    spread = jnp.mean(center * center, axis=-1, keepdims=True)
    return center * lax.rsqrt(spread + epsilon) * gain + shift


def smooth(value):
    return jax.nn.gelu(value, approximate=False)


def matmul(left, right):
    return jnp.dot(left, right, preferred_element_type=jnp.float32)


def matmul_lower(left, right):
    return lax.dot_general(
        left, right, (((0,), (0,)), ((), ())), preferred_element_type=jnp.float32
    )


def matmul_upper(left, right):
    return lax.dot_general(
        left, right, (((1,), (1,)), ((), ())), preferred_element_type=jnp.float32
    )


def scores_of(queries, keys, frames):
    scores = jnp.einsum("bqhd,bkhd->bhqk", queries, keys, preferred_element_type=jnp.float32)
    scores = scores * queries.shape[-1] ** (-0.5)
    allowed = frames[:, None, None, :] <= frames[:, None, :, None]
    return jnp.where(allowed, scores, masked_value)


def attend_group(packed, frames):
    queries, keys, values = (packed[:, :, 0], packed[:, :, 1], packed[:, :, 2])
    scores = scores_of(queries, keys, frames)
    peak = jnp.max(scores, axis=-1, keepdims=True)
    weights = jnp.exp(scores - peak)
    total = jnp.sum(weights, axis=-1, keepdims=True)
    probs = (weights / total).astype(jnp.bfloat16)
    mixed = jnp.einsum("bhqk,bkhd->bqhd", probs, values, preferred_element_type=jnp.float32)
    return (mixed.astype(jnp.bfloat16), (peak + jnp.log(total))[..., 0])


def attend_back(packed, frames, logsum, grad_mixed):
    queries, keys, values = (packed[:, :, 0], packed[:, :, 1], packed[:, :, 2])
    scale = queries.shape[-1] ** (-0.5)
    probs = jnp.exp(scores_of(queries, keys, frames) - logsum[..., None])
    grad_probs = jnp.einsum(
        "bqhd,bkhd->bhqk", grad_mixed, values, preferred_element_type=jnp.float32
    )
    inner = jnp.sum(probs * grad_probs, axis=-1, keepdims=True)
    grad_scores = (probs * (grad_probs - inner)).astype(jnp.bfloat16)
    grad_queries = (
        jnp.einsum("bhqk,bkhd->bqhd", grad_scores, keys, preferred_element_type=jnp.float32) * scale
    )
    grad_keys = (
        jnp.einsum("bhqk,bqhd->bkhd", grad_scores, queries, preferred_element_type=jnp.float32)
        * scale
    )
    grad_values = jnp.einsum(
        "bhqk,bqhd->bkhd",
        probs.astype(jnp.bfloat16),
        grad_mixed,
        preferred_element_type=jnp.float32,
    )
    return jnp.stack([grad_queries, grad_keys, grad_values], axis=2).astype(jnp.bfloat16)


def layer_forward(inputs, frames, weights):
    (
        attend_gain,
        attend_shift,
        inward_weight,
        inward_bias,
        outward_weight,
        outward_bias,
        mixing_gain,
        mixing_shift,
        up_weight,
        up_bias,
        down_weight,
        down_bias,
    ) = weights
    width = inputs.shape[1]
    sequences, length = frames.shape
    normed = normalize(inputs, attend_gain, attend_shift).astype(jnp.bfloat16)
    bias_full = jnp.concatenate(
        [inward_bias[:width], jnp.zeros((width,), jnp.float32), inward_bias[width:]]
    )
    packed = (matmul(normed, inward_weight) + bias_full).astype(jnp.bfloat16)
    grouped = packed.reshape(sequences // 2, 2, length, 3, HEADS, width // HEADS)
    mixed, logsum = lax.map(
        lambda item: attend_group(item[0], item[1]),
        (grouped, frames.reshape(sequences // 2, 2, length)),
    )
    mixed = mixed.reshape(sequences * length, width)
    middle = inputs + matmul(mixed, outward_weight) + outward_bias
    second = normalize(middle, mixing_gain, mixing_shift).astype(jnp.bfloat16)
    raised = matmul(second, up_weight) + up_bias
    activated = smooth(raised).astype(jnp.bfloat16)
    result = middle + matmul(activated, down_weight) + down_bias
    return (result, (normed, packed, mixed, logsum, middle, second, raised, activated))


def backward_inputs(inputs, incoming, frames, weights, kept):
    (
        attend_gain,
        attend_shift,
        inward_weight,
        inward_bias,
        outward_weight,
        outward_bias,
        mixing_gain,
        mixing_shift,
        up_weight,
        up_bias,
        down_weight,
        down_bias,
    ) = weights
    normed, packed, mixed, logsum, middle, second, raised, activated = kept
    width = inputs.shape[1]
    sequences, length = frames.shape
    down_in = incoming.astype(jnp.bfloat16)
    grad_activated = matmul_upper(down_in, down_weight)
    grad_raised = jax.vjp(smooth, raised)[1](grad_activated)[0].astype(jnp.bfloat16)
    grad_second = matmul_upper(grad_raised, up_weight)
    second_back = jax.vjp(normalize, middle, mixing_gain, mixing_shift)[1]
    grad_middle_part, grad_mixing_gain, grad_mixing_shift = second_back(grad_second)
    grad_middle = incoming + grad_middle_part
    outward_in = grad_middle.astype(jnp.bfloat16)
    grad_mixed = matmul_upper(outward_in, outward_weight).astype(jnp.bfloat16)
    grouped = packed.reshape(sequences // 2, 2, length, 3, HEADS, width // HEADS)
    grad_packed = lax.map(
        lambda item: attend_back(item[0], item[1], item[2], item[3]),
        (
            grouped,
            frames.reshape(sequences // 2, 2, length),
            logsum,
            grad_mixed.reshape(sequences // 2, 2, length, HEADS, width // HEADS),
        ),
    )
    grad_packed = grad_packed.reshape(sequences * length, 3 * width)
    grad_normed = matmul_upper(grad_packed, inward_weight)
    first_back = jax.vjp(normalize, inputs, attend_gain, attend_shift)[1]
    grad_input_part, grad_attend_gain, grad_attend_shift = first_back(grad_normed)
    small = (grad_attend_gain, grad_attend_shift, grad_mixing_gain, grad_mixing_shift)
    pieces = (activated, down_in, second, grad_raised, mixed, outward_in, normed, grad_packed)
    return (grad_middle + grad_input_part, small, pieces)


def weight_products(small, pieces):
    activated, down_in, second, grad_raised, mixed, outward_in, normed, grad_packed = pieces
    width = normed.shape[1]
    column = jnp.sum(grad_packed, axis=0, dtype=jnp.float32)
    return (
        small[0],
        small[1],
        matmul_lower(normed, grad_packed),
        jnp.concatenate([column[:width], column[2 * width :]]),
        matmul_lower(mixed, outward_in),
        jnp.sum(outward_in, axis=0, dtype=jnp.float32),
        small[2],
        small[3],
        matmul_lower(second, grad_raised),
        jnp.sum(grad_raised, axis=0, dtype=jnp.float32),
        matmul_lower(activated, down_in),
        jnp.sum(down_in, axis=0, dtype=jnp.float32),
    )


def accumulate(totals, grads):
    return grads if totals is None else tuple((left + right for left, right in zip(totals, grads)))


def body(
    tokens,
    cotangent,
    frame_ids,
    attend_gain,
    attend_shift,
    inward_weight,
    inward_bias,
    outward_weight,
    outward_bias,
    mixing_gain,
    mixing_shift,
    up_weight,
    up_bias,
    down_weight,
    down_bias,
):
    weights = tuple(
        (
            item[0]
            for item in (
                attend_gain,
                attend_shift,
                inward_weight,
                inward_bias,
                outward_weight,
                outward_bias,
                mixing_gain,
                mixing_shift,
                up_weight,
                up_bias,
                down_weight,
                down_bias,
            )
        )
    )
    section = lax.axis_index("section")
    first = section == 0
    sequences, length, width = tokens.shape
    micro = MICRO
    per_micro = sequences // micro
    rows = per_micro * length
    token_parts = tokens.reshape(micro, rows, width)
    tangent_parts = cotangent.reshape(micro, rows, width)
    frame_parts = frame_ids.reshape(micro, per_micro, length)
    received = jnp.zeros((rows, width), jnp.float32)
    section_inputs = []
    results = []
    for tick in range(micro + 1):
        own = token_parts[min(tick, micro - 1)].astype(jnp.float32)
        current = jnp.where(first, own, received)
        frames = frame_parts[jnp.clip(tick - section, 0, micro - 1)]
        result, kept = layer_forward(current, frames, weights)
        section_inputs.append(current)
        results.append(result)
        if tick < micro:
            received = from_behind(result.astype(jnp.bfloat16), "section", 1).astype(jnp.float32)
    received = jnp.zeros((rows, width), jnp.float32)
    totals = None
    grad_ticks = []
    for tick in range(micro + 1):
        own = tangent_parts[min(tick, micro - 1)].astype(jnp.float32)
        incoming = jnp.where(first, received, own)
        member = tick - 1 + section
        valid = ((member >= 0) & (member < micro)).astype(jnp.float32)
        frames = frame_parts[jnp.clip(member, 0, micro - 1)]
        lower_tick = max(tick - 1, 0)
        upper_tick = min(tick + 1, micro)
        current = jnp.where(first, section_inputs[lower_tick], section_inputs[upper_tick])
        kept = layer_forward(current, frames, weights)[1]
        grad_input, small, pieces = backward_inputs(current, incoming, frames, weights, kept)
        grads = tuple((item * valid for item in weight_products(small, pieces)))
        totals = accumulate(totals, grads)
        grad_ticks.append(grad_input)
        if tick < micro:
            received = from_behind(grad_input.astype(jnp.bfloat16), "section", -1).astype(
                jnp.float32
            )
    totals = lax.psum(totals, "batch")
    layer_all = jnp.concatenate(results[1:], axis=0)
    grad_all = jnp.concatenate(grad_ticks[1:], axis=0)
    half = width // 2
    rounded = layer_all.astype(jnp.bfloat16)
    sending = jnp.where(first, grad_all[:, half:], rounded[:, :half].astype(jnp.float32))
    arrived = shifted(sending.astype(jnp.bfloat16), "section", 1).astype(sending.dtype)
    layer_out = jnp.where(first, arrived.astype(jnp.bfloat16), rounded[:, half:])
    input_grad = jnp.where(first, grad_all[:, :half], arrived)
    layer_out = layer_out.reshape(sequences, length, half)
    input_grad = input_grad.reshape(sequences, length, half)
    return (
        layer_out,
        input_grad,
        totals[0][None],
        totals[1][None],
        totals[2][None],
        totals[3][None],
        totals[4][None],
        totals[5][None],
        totals[6][None],
        totals[7][None],
        totals[8][None],
        totals[9][None],
        totals[10][None],
        totals[11][None],
    )


def solution(mesh):
    return jax.shard_map(
        body,
        mesh=mesh,
        in_specs=(
            P("batch", None, None),
            P("batch", None, None),
            P("batch", None),
            P("section", None),
            P("section", None),
            P("section", None, None),
            P("section", None),
            P("section", None, None),
            P("section", None),
            P("section", None),
            P("section", None),
            P("section", None, None),
            P("section", None),
            P("section", None, None),
            P("section", None),
        ),
        out_specs=(
            P("batch", None, "section"),
            P("batch", None, "section"),
            P("section", None),
            P("section", None),
            P("section", None, None),
            P("section", None),
            P("section", None, None),
            P("section", None),
            P("section", None),
            P("section", None),
            P("section", None, None),
            P("section", None),
            P("section", None, None),
            P("section", None),
        ),
        check_vma=False,
    )
```

profile of v0, /device:TPU:0, one launch (start us, length us, event | category | flops | bytes accessed | tf_op | source)
XLA Modules:
  0.0 1205.4 jit_solution(16951399746607520137)
XLA Ops:
  10.7 8.4 convert_reduce_fusion.19
  31.1 7.4 copy.201
  38.9 18.2 %while.160 = (s32[]{:T(128)}, bf16[2,2,357,4,64]{2,1,0,4,3:T(2,128)(2,1)S(1)}, bf16[2,2,357,3,4,64]{2,5,4,1,3,0:T(8,128)(2,1)}, s32[2,2,357]{2,1,0:T(2,128)S(1)}, s32[]{:T(128)}) while((s32[]{:T(128)}, bf16[2,2,357,4,64]{2,1,0,4,3:T(2,128)(2,1)S(1)}, bf16[2,2,357,3,4,64]{2,5,4,1,3,0:T(8,128)(2,1)}, s32[2,2,357]{2,1,0:T(2,128)S(1)}, ...), condition=%wide.region_5.6_spmd, body=%wide.region_2.5_spmd.sunk | while | flops 267571136 | bytes 13245531 | solution.py:118
  61.4 14.6 %fusion.340 = bf16[1428,256]{1,0:T(8,128)(2,1)} fusion(f32[1428,256]{1,0:T(8,128)S(1)} %get-tuple-element.1040, f32[1024]{0:T(1024)S(1)} %bitcast.1079, f32[256]{0:T(256)S(1)} %bitcast.1160, f32[256]{0:T(256)S(1)} %bitcast.1095, f32[256]{0:T(256)S(1)} %bitcast.1044, f32[1428]{0:T(1024)S(1)} %add_rsqrt_fusion.9, f32[1428]{0:T(1024)S(1)} %broadcast_multiply_fusion.19, ...), kind=kOutput, calls=%fused_computation.622 | convolution fusion | flops 1596801024 | bytes 3260576 | tf_op jit(solution)/shard_map/dot_general | solution.py:37
  118.2 7.5 reshape.1212
  125.7 7.4 copy.214
  134.3 24.2 %while.163 = (s32[]{:T(128)}, bf16[2,2,357,4,64]{2,1,0,4,3:T(2,128)(2,1)}, bf16[2,2,357,3,4,64]{2,5,4,1,3,0:T(8,128)(2,1)}, s32[2,2,357]{2,1,0:T(2,128)S(1)}, s32[]{:T(128)}) while((s32[]{:T(128)}, bf16[2,2,357,4,64]{2,1,0,4,3:T(2,128)(2,1)}, bf16[2,2,357,3,4,64]{2,5,4,1,3,0:T(8,128)(2,1)}, s32[2,2,357]{2,1,0:T(2,128)S(1)}, ...), condition=%wide.region_28.29_spmd, body=%wide.region_25.28_spmd.sunk | while | flops 267571136 | bytes 19417540 | solution.py:118
  162.8 17.3 %fusion.339 = bf16[1428,256]{1,0:T(8,128)(2,1)} fusion(f32[1428,256]{1,0:T(8,128)} %copy-done.105, f32[1024]{0:T(1024)S(1)} %bitcast.1080, f32[1428]{0:T(1024)S(1)} %add_rsqrt_fusion.7, f32[1428]{0:T(1024)S(1)} %broadcast_multiply_fusion.15, f32[256]{0:T(256)S(1)} %bitcast.1161, f32[256]{0:T(256)S(1)} %bitcast.1096, f32[256]{0:T(256)S(1)} %bitcast.1045, ...), kind=kOutput, calls=%fused_computation.621 | convolution fusion | flops 1596801024 | bytes 3260576 | tf_op jit(solution)/shard_map/dot_general | solution.py:37
  185.8 7.4 reshape.1220
  205.7 7.3 reshape.1214
  213.0 7.4 copy.226
  221.6 24.1 %while.166 = (s32[]{:T(128)}, bf16[2,2,357,4,64]{2,1,0,4,3:T(2,128)(2,1)}, bf16[2,2,357,3,4,64]{2,5,4,1,3,0:T(8,128)(2,1)}, s32[2,2,357]{2,1,0:T(2,128)S(1)}, s32[]{:T(128)}) while((s32[]{:T(128)}, bf16[2,2,357,4,64]{2,1,0,4,3:T(2,128)(2,1)}, bf16[2,2,357,3,4,64]{2,5,4,1,3,0:T(8,128)(2,1)}, s32[2,2,357]{2,1,0:T(2,128)S(1)}, ...), condition=%wide.region_51.52_spmd, body=%wide.region_48.51_spmd.sunk | while | flops 267571136 | bytes 19417540 | solution.py:118
  252.8 17.1 %fusion.338 = bf16[1428,256]{1,0:T(8,128)(2,1)} fusion(f32[1428,256]{1,0:T(8,128)} %copy-done.106, f32[1024]{0:T(1024)S(1)} %bitcast.1081, f32[1428]{0:T(1024)S(1)} %add_rsqrt_fusion.5, f32[1428]{0:T(1024)S(1)} %broadcast_multiply_fusion.11, f32[256]{0:T(256)S(1)} %bitcast.1162, f32[256]{0:T(256)S(1)} %bitcast.1097, f32[256]{0:T(256)S(1)} %bitcast.1046, ...), kind=kOutput, calls=%fused_computation.620 | convolution fusion | flops 1596801024 | bytes 3260576 | tf_op jit(solution)/shard_map/dot_general | solution.py:37
  273.7 11.3 while.161
  300.6 7.4 copy.237
  308.5 17.9 %while.169 = (s32[]{:T(128)}, bf16[2,2,357,4,64]{2,1,0,4,3:T(2,128)(2,1)S(1)}, bf16[2,2,357,3,4,64]{2,5,4,1,3,0:T(8,128)(2,1)}, s32[2,2,357]{2,1,0:T(2,128)S(1)}, s32[]{:T(128)}) while((s32[]{:T(128)}, bf16[2,2,357,4,64]{2,1,0,4,3:T(2,128)(2,1)S(1)}, bf16[2,2,357,3,4,64]{2,5,4,1,3,0:T(8,128)(2,1)}, s32[2,2,357]{2,1,0:T(2,128)S(1)}, ...), condition=%wide.region_74.75_spmd, body=%wide.region_71.74_spmd.sunk | while | flops 267571136 | bytes 13245531 | solution.py:118
  330.0 15.9 %fusion.337 = bf16[1428,256]{1,0:T(8,128)(2,1)S(1)} fusion(f32[1428,256]{1,0:T(8,128)} %copy-done.107, f32[1024]{0:T(1024)S(1)} %bitcast.1082, f32[1428]{0:T(1024)S(1)} %add_rsqrt_fusion.3, f32[1428]{0:T(1024)S(1)} %broadcast_multiply_fusion.7, f32[256]{0:T(256)S(1)} %bitcast.1163, f32[256]{0:T(256)S(1)} %bitcast.1098, f32[256]{0:T(256)S(1)} %bitcast.1047, ...), kind=kOutput, calls=%fused_computation.619 | convolution fusion | flops 1596801024 | bytes 3260576 | tf_op jit(solution)/shard_map/dot_general | solution.py:37
  351.2 11.3 collective-permute-done.6
  381.9 10.9 while.172
  414.9 11.1 while.167
  447.4 11.1 while.170
  479.9 11.3 while.164
  507.3 70.5 %fusion.241 = (f32[1428,1024]{1,0:T(8,128)}, f32[1428,1024]{1,0:T(8,128)}, f32[1428,1024]{1,0:T(8,128)}, f32[1428,1024]{1,0:T(8,128)}, f32[1428,1024]{1,0:T(8,128)S(1)}, /*index=5*/f32[1428,1024]{1,0:T(8,128)}) fusion(f32[1024]{0:T(1024)S(1)} %bitcast.1083, f32[1428,1024]{1,0:T(8,128)S(1)} %fusion.445, f32[1428,1024]{1,0:T(8,128)S(1)} %fusion.451, ...), kind=kOutput, calls=%fused_computation.391 | convolution fusion | flops 1211126784 | bytes 60495008 | tf_op jit(solution)/shard_map/dot_general | solution.py:37
  596.4 18.6 %while.162 = (s32[]{:T(128)}, bf16[2,2,357,3,4,64]{2,5,4,1,3,0:T(8,128)(2,1)}, bf16[2,2,357,3,4,64]{2,5,4,1,3,0:T(8,128)(2,1)S(1)}, s32[2,2,357]{2,1,0:T(2,128)S...) while((s32[]{:T(128)}, ...), condition=%wide.region_20.21_spmd, body=%wide.region_18.20_spmd.sunk | while | flops 672288832 | bytes 61650632 | solution.py:159
  622.4 7.1 reshape.1177
  642.7 7.4 copy.254
  650.5 17.8 %while.174 = (s32[]{:T(128)}, bf16[2,2,357,4,64]{2,1,0,4,3:T(2,128)(2,1)S(1)}, bf16[2,2,357,3,4,64]{2,5,4,1,3,0:T(8,128)(2,1)}, s32[2,2,357]{2,1,0:T(2,128)S(1)}, s32[]{:T(128)}) while((s32[]{:T(128)}, bf16[2,2,357,4,64]{2,1,0,4,3:T(2,128)(2,1)S(1)}, bf16[2,2,357,3,4,64]{2,5,4,1,3,0:T(8,128)(2,1)}, s32[2,2,357]{2,1,0:T(2,128)S(1)}, ...), condition=%wide.region_112.113_spmd, body=%wide.region_109.112_spmd.sunk | while | flops 267571136 | bytes 13245531 | solution.py:118
  672.1 17.1 %fusion.336 = bf16[1428,256]{1,0:T(8,128)(2,1)} fusion(f32[1428,256]{1,0:T(8,128)} %copy-done.104, f32[1024]{0:T(1024)S(1)} %bitcast.1085, f32[1428]{0:T(1024)S(1)} %add_rsqrt_fusion.1, f32[1428]{0:T(1024)S(1)} %broadcast_multiply_fusion.1, f32[256]{0:T(256)S(1)} %bitcast.1164, f32[256]{0:T(256)S(1)} %bitcast.1104, f32[256]{0:T(256)S(1)} %bitcast.1055, ...), kind=kOutput, calls=%fused_computation.618 | convolution fusion | flops 1596801024 | bytes 3260576 | tf_op jit(solution)/shard_map/dot_general | solution.py:37
  694.5 17.2 %concatenate.76 = bf16[5712,256]{1,0:T(8,128)(2,1)} concatenate(bf16[1428,256]{1,0:T(8,128)(2,1)} %fusion.339, bf16[1428,256]{1,0:T(8,128)(2,1)} %fusion.338, bf16[1428,256]{1,0:T(8,128)(2,1)} %copy-done.142, bf16[1428,256]{1,0:T(8,128)(2,1)} %fusion.336), dimensions={0} | concatenate | bytes 5849088 | tf_op jit(solution)/shard_map/concatenate | solution.py:280
  713.1 7.7 fusion.345
  744.3 18.7 %while.165 = (s32[]{:T(128)}, bf16[2,2,357,3,4,64]{2,5,4,1,3,0:T(8,128)(2,1)}, bf16[2,2,357,3,4,64]{2,5,4,1,3,0:T(8,128)(2,1)S(1)}, s32[2,2,357]{2,1,0:T(2,128)S...) while((s32[]{:T(128)}, ...), condition=%wide.region_43.44_spmd, body=%wide.region_41.43_spmd.sunk | while | flops 672288832 | bytes 61650632 | solution.py:159
  771.6 7.3 reshape.1183
  797.7 10.5 collective-permute-done.3
  832.0 18.6 %while.168 = (s32[]{:T(128)}, bf16[2,2,357,3,4,64]{2,5,4,1,3,0:T(8,128)(2,1)}, bf16[2,2,357,3,4,64]{2,5,4,1,3,0:T(8,128)(2,1)S(1)}, s32[2,2,357]{2,1,0:T(2,128)S...) while((s32[]{:T(128)}, ...), condition=%wide.region_66.67_spmd, body=%wide.region_64.66_spmd.sunk | while | flops 672288832 | bytes 61650632 | solution.py:159
  861.1 6.8 reshape.1189
  879.5 7.4 fusion.343
  887.0 8.4 collective-permute-done.5
  919.4 18.5 %while.171 = (s32[]{:T(128)}, bf16[2,2,357,3,4,64]{2,5,4,1,3,0:T(8,128)(2,1)}, bf16[2,2,357,3,4,64]{2,5,4,1,3,0:T(8,128)(2,1)S(1)}, s32[2,2,357]{2,1,0:T(2,128)S...) while((s32[]{:T(128)}, ...), condition=%wide.region_89.90_spmd, body=%wide.region_87.89_spmd.sunk | while | flops 672288832 | bytes 61650632 | solution.py:159
  949.0 6.8 reshape.1195
  967.4 7.4 fusion.342
  974.8 7.5 collective-permute-done.7
  1004.7 18.8 %while.173 = (s32[]{:T(128)}, bf16[2,2,357,3,4,64]{2,5,4,1,3,0:T(8,128)(2,1)}, bf16[2,2,357,3,4,64]{2,5,4,1,3,0:T(8,128)(2,1)S(1)}, s32[2,2,357]{2,1,0:T(2,128)S...) while((s32[]{:T(128)}, ...), condition=%wide.region_104.105_spmd, body=%wide.region_102.104_spmd.sunk | while | flops 672288832 | bytes 61650632 | solution.py:159
  1029.8 7.3 fusion.341
  1040.6 6.8 reshape.1199
  1056.0 18.5 %concatenate.75 = f32[5712,256]{1,0:T(8,128)} concatenate(f32[1428,256]{1,0:T(8,128)} %get-tuple-element.948, f32[1428,256]{1,0:T(8,128)} %get-tuple-element.938, f32[1428,256]{1,0:T(8,128)} %get-tuple-element.930, f32[1428,256]{1,0:T(8,128)} %add_add_fusion.10), dimensions={0} | concatenate | bytes 11698176 | tf_op jit(solution)/shard_map/concatenate | solution.py:281
  1077.9 7.2 fusion.355
  1089.1 58.7 %all-reduce = (f32[1,256]{1,0:T(1,128)}, f32[1,256]{1,0:T(1,128)}, f32[1,512]{1,0:T(1,128)}, f32[1,256]{1,0:T(1,128)}, f32[1,256]{1,0:T(1,128)}, /*index=5*/f32[...) all-reduce(f32[1,256]{1,0:T(1,128)S(1)} %bitcast.1142, ...), channel_id=1, replica_groups=mesh['section'=2,'batch'=16] {'batch'}, use_global_device_ids=true, to_apply=%region_120.121 | all-reduce | flops 3072 | bytes 24576 | tf_op jit(solution)/shard_map/psum | solution.py:279
  1161.4 29.9 %all-reduce.4.cloned.1.call-done = (f32[1,256,768]{2,1,0:T(8,128)}, f32[1,256,256]{2,1,0:T(8,128)}, f32[1,256,1024]{2,1,0:T(8,128)}, f32[1,1024,256]{2,1,0:T(8,128)}) async-done(((f32[1,256,768]{2,1,0:T(8,128)}, f32[1,256,256]{2,1,0:T(8,128)}, f32[1,256,1024]{2,1,0:T(8,128)}, f32[1,1024,256]{2,1,0:T(8,128)}), (f32[1,256,768]{2,1,0:T(8,128)}, f32[1,256,256]{2,1,0:T(8,128)}, f32[1,256,1024]{2,1,0:T(8,128)}, ...) | async-done | bytes 3145744 | tf_op jit(solution)/shard_map/psum | solution.py:279
  (1259 shorter events, 728.9 us)
Async XLA Ops:
  7.2 54.1 %copy-start = (bf16[1,256,1024]{2,1,0:T(8,128)(2,1)S(1)}, bf16[1,256,1024]{2,1,0:T(8,128)(2,1)}, u32[]{:S(2)}) copy-start(bf16[1,256,1024]{2,1,0:T(8,128)(2,1)} %param.56) | copy-start | bytes 1572868
  7.2 1184.1 %all-reduce.4.cloned.1.call-start = ((), (), s32[]{:S(2)}) async-start(), calls=%async_computation | async-start | bytes 6291456 | tf_op jit(solution)/shard_map/psum | solution.py:279
  38.8 19.7 %copy-start.31 = (bf16[1,256,256]{2,1,0:T(8,128)(2,1)S(1)}, bf16[1,256,256]{2,1,0:T(8,128)(2,1)}, u32[]{:S(2)}) copy-start(bf16[1,256,256]{2,1,0:T(8,128)(2,1)} %param.52) | copy-start | bytes 393220
  38.9 19.7 %copy-start.184 = (f32[1,256]{1,0:T(1,128)S(1)}, f32[1,256]{1,0:T(1,128)}, u32[]{:S(2)}) copy-start(f32[1,256]{1,0:T(1,128)} %param.53) | copy-start | bytes 3076
  76.0 34.6 %collective-permute-start = (bf16[1428,256]{1,0:T(8,128)(2,1)}, bf16[1428,256]{1,0:T(8,128)(2,1)}, u32[]{:S(2)}, u32[]{:S(2)}) collective-permute-start(bf16[1428,256]{1,0:T(8,128)(2,1)} %fusion.340), channel_id=1, source_target_pairs={{0,16},{1,17},{2,18},{3,19},{4,20},{5,21},{6,22},{7,23},{8,24},{9,... | collective-permute-start | bytes 2193416 | tf_op jit(solution)/shard_map/ppermute | solution.py:17
  113.9 47.2 %copy-start.16 = (f32[1428,256]{1,0:T(8,128)}, f32[1428,256]{1,0:T(8,128)S(1)}, u32[]{:S(2)}) copy-start(f32[1428,256]{1,0:T(8,128)S(1)} %get-tuple-element.963) | copy-start | bytes 4386820
  162.7 19.5 %copy-start.38 = (f32[1428,256]{1,0:T(8,128)S(1)}, f32[1428,256]{1,0:T(8,128)}, u32[]{:S(2)}) copy-start(f32[1428,256]{1,0:T(8,128)} %get-tuple-element.962) | copy-start | bytes 4386820
  162.7 20.0 %copy-start.277 = (bf16[1,256,768]{2,1,0:T(8,128)(2,1)S(1)}, bf16[1,256,768]{2,1,0:T(8,128)(2,1)}, u32[]{:S(2)}) copy-start(bf16[1,256,768]{2,1,0:T(8,128)(2,1)} %param.50) | copy-start | bytes 1179652
  180.1 19.6 %collective-permute-start.2 = (bf16[1428,256]{1,0:T(8,128)(2,1)}, bf16[1428,256]{1,0:T(8,128)(2,1)}, u32[]{:S(2)}, u32[]{:S(2)}) collective-permute-start(bf16[1428,256]{1,0:T(8,128)(2,1)} %fusion.339), channel_id=1, source_target_pairs={{0,16},{1,17},{2,18},{3,19},{4,20},{5,21},{6,22},{7,23},{8,24},{9,... | collective-permute-start | bytes 2193416 | tf_op jit(solution)/shard_map/ppermute | solution.py:17
  252.8 20.9 %copy-start.171 = (s32[2,2,357]{2,1,0:T(2,128)S(1)}, s32[2,2,357]{2,1,0:T(2,128)}, u32[]{:S(2)}) copy-start(s32[2,2,357]{2,1,0:T(2,128)} %reshape_squeeze.36) | copy-start | bytes 17140
  270.0 22.0 %collective-permute-start.4 = (bf16[1428,256]{1,0:T(8,128)(2,1)}, bf16[1428,256]{1,0:T(8,128)(2,1)}, u32[]{:S(2)}, u32[]{:S(2)}) collective-permute-start(bf16[1428,256]{1,0:T(8,128)(2,1)} %fusion.338), channel_id=1, source_target_pairs={{0,16},{1,17},{2,18},{3,19},{4,20},{5,21},{6,22},{7,23},{8,24},{9,... | collective-permute-start | bytes 2193416 | tf_op jit(solution)/shard_map/ppermute | solution.py:17
  291.9 55.7 %copy-start.154 = (f32[1428]{0:T(1024)}, f32[1428]{0:T(1024)S(1)}, u32[]{:S(2)}) copy-start(f32[1428]{0:T(1024)S(1)} %broadcast_multiply_fusion.17) | copy-start | bytes 17140
  329.9 17.2 %copy-start.18 = (f32[1428,256]{1,0:T(8,128)S(1)}, f32[1428,256]{1,0:T(8,128)}, u32[]{:S(2)}) copy-start(f32[1428,256]{1,0:T(8,128)} %get-tuple-element.1056) | copy-start | bytes 4386820
  345.8 16.7 %collective-permute-start.6 = (bf16[1428,256]{1,0:T(8,128)(2,1)S(1)}, bf16[1428,256]{1,0:T(8,128)(2,1)S(1)}, u32[]{:S(2)}, u32[]{:S(2)}) collective-permute-start(bf16[1428,256]{1,0:T(8,128)(2,1)S(1)} %fusion.337), channel_id=1, source_target_pairs={{0,16},{1,17},{2,18},{3,19},{4,20},{5,21},{6,22},{7,23},{8,24},{9,... | collective-permute-start | bytes 2193416 | tf_op jit(solution)/shard_map/ppermute | solution.py:17
  347.7 14.8 %copy-start.90 = (f32[1428,256]{1,0:T(8,128)S(1)}, f32[1428,256]{1,0:T(8,128)}, u32[]{:S(2)}) copy-start(f32[1428,256]{1,0:T(8,128)} %reshape.1208) | copy-start | bytes 4386820
  347.7 15.1 %copy-start.49 = (f32[1428,256]{1,0:T(8,128)S(1)}, f32[1428,256]{1,0:T(8,128)}, u32[]{:S(2)}) copy-start(f32[1428,256]{1,0:T(8,128)} %copy-done.48) | copy-start | bytes 4386820
  347.7 15.1 %copy-start.58 = (f32[1428,256]{1,0:T(8,128)S(1)}, f32[1428,256]{1,0:T(8,128)}, u32[]{:S(2)}) copy-start(f32[1428,256]{1,0:T(8,128)} %copy-done.57) | copy-start | bytes 4386820
  364.5 36.7 %copy-start.197 = (f32[1428]{0:T(1024)}, f32[1428]{0:T(1024)S(1)}, u32[]{:S(2)}) copy-start(f32[1428]{0:T(1024)S(1)} %broadcast_multiply_fusion.10) | copy-start | bytes 17140
  364.5 69.1 %copy-start.195 = (f32[1428]{0:T(1024)}, f32[1428]{0:T(1024)S(1)}, u32[]{:S(2)}) copy-start(f32[1428]{0:T(1024)S(1)} %broadcast_multiply_fusion.6) | copy-start | bytes 17140
  366.6 67.0 %copy-start.234 = (f32[1428]{0:T(1024)}, f32[1428]{0:T(1024)S(1)}, u32[]{:S(2)}) copy-start(f32[1428]{0:T(1024)S(1)} %fusion.511) | copy-start | bytes 17140
  367.2 34.0 %copy-start.236 = (f32[1428]{0:T(1024)}, f32[1428]{0:T(1024)S(1)}, u32[]{:S(2)}) copy-start(f32[1428]{0:T(1024)S(1)} %fusion.509) | copy-start | bytes 17140
  432.0 68.7 %copy-start.159 = (f32[1428]{0:T(1024)}, f32[1428]{0:T(1024)S(1)}, u32[]{:S(2)}) copy-start(f32[1428]{0:T(1024)S(1)} %broadcast_multiply_fusion.9) | copy-start | bytes 17140
  433.6 67.0 %copy-start.178 = (f32[1428]{0:T(1024)}, f32[1428]{0:T(1024)S(1)}, u32[]{:S(2)}) copy-start(f32[1428]{0:T(1024)S(1)} %fusion.510) | copy-start | bytes 17140
  464.5 34.8 %copy-start.157 = (f32[1428]{0:T(1024)}, f32[1428]{0:T(1024)S(1)}, u32[]{:S(2)}) copy-start(f32[1428]{0:T(1024)S(1)} %broadcast_multiply_fusion.5) | copy-start | bytes 17140
  466.2 33.1 %copy-start.173 = (f32[1428]{0:T(1024)}, f32[1428]{0:T(1024)S(1)}, u32[]{:S(2)}) copy-start(f32[1428]{0:T(1024)S(1)} %fusion.512) | copy-start | bytes 17140
  507.2 70.6 %copy-start.13 = (f32[1428,1024]{1,0:T(8,128)}, f32[1428,1024]{1,0:T(8,128)S(1)}, u32[]{:S(2)}) copy-start(f32[1428,1024]{1,0:T(8,128)S(1)} %fusion.451) | copy-start | bytes 17547268
  507.3 70.6 %copy-start.141 = (bf16[1428,256]{1,0:T(8,128)(2,1)S(1)}, bf16[1428,256]{1,0:T(8,128)(2,1)}, u32[]{:S(2)}) copy-start(bf16[1428,256]{1,0:T(8,128)(2,1)} %convert_element_type.555) | copy-start | bytes 2193412
  507.3 70.6 %copy-start.271 = (bf16[1,1024,256]{2,1,0:T(8,128)(2,1)S(1)}, bf16[1,1024,256]{2,1,0:T(8,128)(2,1)}, u32[]{:S(2)}) copy-start(bf16[1,1024,256]{2,1,0:T(8,128)(2,1)} %param.58) | copy-start | bytes 1572868
  650.5 18.4 %copy-start.185 = (f32[1,256]{1,0:T(1,128)S(1)}, f32[1,256]{1,0:T(1,128)}, u32[]{:S(2)}) copy-start(f32[1,256]{1,0:T(1,128)} %param.53) | copy-start | bytes 3076
  672.1 17.1 %copy-start.215 = (f32[1428]{0:T(1024)S(1)}, f32[1428]{0:T(1024)}, u32[]{:S(2)}) copy-start(f32[1428]{0:T(1024)} %copy-done.214) | copy-start | bytes 17140
  672.1 17.1 %copy-start.40 = (f32[1428,256]{1,0:T(8,128)S(1)}, f32[1428,256]{1,0:T(8,128)}, u32[]{:S(2)}) copy-start(f32[1428,256]{1,0:T(8,128)} %get-tuple-element.962) | copy-start | bytes 4386820
  693.2 27.6 %collective-permute-start.1 = (bf16[1428,256]{1,0:T(8,128)(2,1)}, bf16[1428,256]{1,0:T(8,128)(2,1)}, u32[]{:S(2)}, u32[]{:S(2)}) collective-permute-start(bf16[1428,256]{1,0:T(8,128)(2,1)} %add_convert_fusion.31), channel_id=1, source_target_pairs={{16,0},{17,1},{18,2},{19,3},{20,4},{21,5},{22,6},{23,7},{24,8},{25... | collective-permute-start | bytes 2193416 | tf_op jit(solution)/shard_map/ppermute | solution.py:17
  694.5 28.2 %slice-start = ((s8[5865472]{0:T(1024)(128)(4,1)}), s8[1671168]{0:T(1024)(128)(4,1)S(1)}, s32[]{:S(2)}) async-start(s8[5865472]{0:T(1024)(128)(4,1)} %bitcast.1034), calls=%async_computation.1 | async-start | bytes 3342336
  786.4 23.7 %slice-start.4 = ((s8[5865472]{0:T(1024)(128)(4,1)}), s8[1671168]{0:T(1024)(128)(4,1)S(1)}, s32[]{:S(2)}) async-start(s8[5865472]{0:T(1024)(128)(4,1)} %bitcast.1038), calls=%async_computation.5 | async-start | bytes 3342336
  788.0 20.1 %collective-permute-start.3 = (bf16[1428,256]{1,0:T(8,128)(2,1)}, bf16[1428,256]{1,0:T(8,128)(2,1)}, u32[]{:S(2)}, u32[]{:S(2)}) collective-permute-start(bf16[1428,256]{1,0:T(8,128)(2,1)} %get-tuple-element.947), channel_id=1, source_target_pairs={{16,0},{17,1},{18,2},{19,3},{20,4},{21,5},{22,6},{23,7},{24,8},{25... | collective-permute-start | bytes 2193416 | tf_op jit(solution)/shard_map/ppermute | solution.py:17
  792.6 15.6 %copy-start.85 = (f32[1428,256]{1,0:T(8,128)S(1)}, f32[1428,256]{1,0:T(8,128)}, u32[]{:S(2)}) copy-start(f32[1428,256]{1,0:T(8,128)} %reshape.1207) | copy-start | bytes 4386820
  792.6 17.5 %slice-start.5 = ((s8[5865472]{0:T(1024)(128)(4,1)}), s8[4194304]{0:T(1024)(128)(4,1)S(1)}, s32[]{:S(2)}) async-start(s8[5865472]{0:T(1024)(128)(4,1)} %bitcast.1038), calls=%async_computation.6 | async-start | bytes 8388608
  797.7 12.4 %copy-start.273 = (bf16[1,1024,256]{2,1,0:T(8,128)(2,1)S(1)}, bf16[1,1024,256]{2,1,0:T(8,128)(2,1)}, u32[]{:S(2)}) copy-start(bf16[1,1024,256]{2,1,0:T(8,128)(2,1)} %param.58) | copy-start | bytes 1572868
  875.4 22.0 %slice-start.2 = ((s8[5865472]{0:T(1024)(128)(4,1)}), s8[1671168]{0:T(1024)(128)(4,1)S(1)}, s32[]{:S(2)}) async-start(s8[5865472]{0:T(1024)(128)(4,1)} %bitcast.1036), calls=%async_computation.3 | async-start | bytes 3342336
  877.0 18.4 %collective-permute-start.5 = (bf16[1428,256]{1,0:T(8,128)(2,1)}, bf16[1428,256]{1,0:T(8,128)(2,1)}, u32[]{:S(2)}, u32[]{:S(2)}) collective-permute-start(bf16[1428,256]{1,0:T(8,128)(2,1)} %get-tuple-element.937), channel_id=1, source_target_pairs={{16,0},{17,1},{18,2},{19,3},{20,4},{21,5},{22,6},{23,7},{24,8},{25... | collective-permute-start | bytes 2193416 | tf_op jit(solution)/shard_map/ppermute | solution.py:17
  879.5 15.8 %copy-start.14 = (f32[1428,256]{1,0:T(8,128)S(1)}, f32[1428,256]{1,0:T(8,128)}, u32[]{:S(2)}) copy-start(f32[1428,256]{1,0:T(8,128)} %reshape.1209) | copy-start | bytes 4386820
  879.5 17.9 %slice-start.3 = ((s8[5865472]{0:T(1024)(128)(4,1)}), s8[4194304]{0:T(1024)(128)(4,1)S(1)}, s32[]{:S(2)}) async-start(s8[5865472]{0:T(1024)(128)(4,1)} %bitcast.1036), calls=%async_computation.4 | async-start | bytes 8388608
  963.2 20.5 %slice-start.8 = ((s8[5865472]{0:T(1024)(128)(4,1)}), s8[1671168]{0:T(1024)(128)(4,1)S(1)}, s32[]{:S(2)}) async-start(s8[5865472]{0:T(1024)(128)(4,1)} %bitcast.1042), calls=%async_computation.9 | async-start | bytes 3342336
  964.9 17.4 %collective-permute-start.7 = (bf16[1428,256]{1,0:T(8,128)(2,1)}, bf16[1428,256]{1,0:T(8,128)(2,1)}, u32[]{:S(2)}, u32[]{:S(2)}) collective-permute-start(bf16[1428,256]{1,0:T(8,128)(2,1)} %get-tuple-element.929), channel_id=1, source_target_pairs={{16,0},{17,1},{18,2},{19,3},{20,4},{21,5},{22,6},{23,7},{24,8},{25... | collective-permute-start | bytes 2193416 | tf_op jit(solution)/shard_map/ppermute | solution.py:17
  967.4 14.9 %copy-start.15 = (f32[1428,256]{1,0:T(8,128)S(1)}, f32[1428,256]{1,0:T(8,128)}, u32[]{:S(2)}) copy-start(f32[1428,256]{1,0:T(8,128)} %reshape.1209) | copy-start | bytes 4386820
  967.4 16.4 %slice-start.9 = ((s8[5865472]{0:T(1024)(128)(4,1)}), s8[4194304]{0:T(1024)(128)(4,1)S(1)}, s32[]{:S(2)}) async-start(s8[5865472]{0:T(1024)(128)(4,1)} %bitcast.1042), calls=%async_computation.10 | async-start | bytes 8388608
  1056.0 18.5 %copy-start.91 = (bf16[5712,256]{1,0:T(8,128)(2,1)S(1)}, bf16[5712,256]{1,0:T(8,128)(2,1)}, u32[]{:S(2)}) copy-start(bf16[5712,256]{1,0:T(8,128)(2,1)} %concatenate.76) | copy-start | bytes 8773636
  1077.9 69.8 %collective-permute-start.8 = (bf16[5712,128]{1,0:T(8,128)(2,1)}, bf16[5712,128]{1,0:T(8,128)(2,1)}, u32[]{:S(2)}, u32[]{:S(2)}) collective-permute-start(bf16[5712,128]{1,0:T(8,128)(2,1)} %fusion.320), channel_id=1, source_target_pairs={{16,0},{0,16},{17,1},{1,17},{18,2},{2,18},{19,3},{3,19},{20,4},{4,... | collective-permute-start | bytes 4386824 | tf_op jit(solution)/shard_map/ppermute | solution.py:23
  (305 other events, 1170.4 us)
Sparse Core Ops, SparseCore 0:
  1085.5 105.7 all-reduce.3
where the time goes:
time: 1220 us; the launch traced here: 1210 us
  matrix products  487 us (40%)
  local copies, waits for them, and re-layouts  423 us (35%)
  other arithmetic  129 us (11%)
  waiting for transfers between devices  67.6 us (6%)
  blocking collectives  58.7 us (5%)
  between operations  17.6 us (1%)
  starting transfers between devices  16.8 us (1%)
    dot_general x30, matrix products, matmul(): return jnp.dot(left, right, preferred_element_type=jnp.float32)  201 us
    dot_general x20, matrix products, matmul_lower(): lax.dot_general(left, right, (((0,), (0,)), ((), ())), preferred_element_...  72.9 us
    while x10, local copies, waits for them, and re-layouts, layer_forward(): lax.map(lambda item: attend_group(item[0], item[1]), (grouped, frames.res...  69.2 us
    dot_general x20, matrix products, matmul_upper(): lax.dot_general(left, right, (((1,), (1,)), ((), ())), preferred_element_...  61.9 us
    psum x1, blocking collectives, body(): totals = lax.psum(totals, 'batch')  58.7 us
    reshape x10, local copies, waits for them, and re-layouts, layer_forward(): packed.reshape(sequences // 2, 2, length, 3, HEADS, width // HEADS)  52.9 us
    dot_general x20, matrix products, attend_group(): jnp.einsum('bhqk,bkhd->bqhd', probs, values, preferred_element_type=jnp.f...  43.9 us
    sub x10, matrix products, attend_group(): weights = jnp.exp(scores - peak)  43.5 us
  transfers between devices with their start and end apart: 10, of which 5 were waited for; matrix products, arithmetic and copies ran while one was open for 12% of the time, Pallas kernels for 0%

commit v1 on v0

v1 whole, which is shorter than its diff:
```python
import functools
from types import SimpleNamespace

import jax
import jax.numpy as jnp
from jax import lax
from jax.experimental import pallas as pl
from jax.experimental.layout import Layout, with_layout_constraint
from jax.experimental.pallas import tpu as pltpu
from jax.sharding import PartitionSpec as P

HEADS = 4
WHOLE_FRAME = 17

epsilon = 1e-05
masked_value = -1e30
log2e = 1.4426950408889634

PAIR = 2
LIVE = 368
ROWS = 384
BOTH = PAIR * ROWS
USED = BOTH - ROWS + LIVE
ONES = 16
STEP = 48
CHUNKS = tuple((at, min(STEP, LIVE - at)) for at in range(0, LIVE, STEP))
MEMBERS = tuple(range(PAIR))
TILES = ((0, 144, 0), (128, 272, 128), (256, 368, 256))
STACK = (0, 144, 416)
STACKED = 784

bf16 = jnp.bfloat16
f32 = jnp.float32


def dot(left, right):
    return jnp.dot(left, right, preferred_element_type=f32)


def dot_upper(left, right):
    return lax.dot_general(left, right, (((1,), (1,)), ((), ())), preferred_element_type=f32)


def gelu_pair(value):
    half = 0.5 + 0.5 * lax.erf(value * 0.7071067811865476)
    bell = jnp.exp2(value * value * (-0.5 * log2e) - 1.3257480647361595)
    return value * half, half + value * bell


def tree(op, parts):
    parts = list(parts)
    while len(parts) > 1:
        pairs = [op(a, b) for a, b in zip(parts[0::2], parts[1::2])]
        parts = pairs + parts[len(parts) // 2 * 2 :]
    return parts[0]


def eights(value):
    return [value[at : at + 8] for at in range(0, value.shape[0], 8)]


def twice(stat):
    return jnp.concatenate([stat, stat], axis=1)


def row_mean(value):
    mean = jnp.mean(value, axis=-1, keepdims=True)
    return jnp.broadcast_to(mean, (value.shape[0], 128))


def normalize(load, T, scales, store):
    for _, _, _, rows in chunks():
        T.mean[rows, :] = row_mean(load(rows))
    for _, _, _, rows in chunks():
        center = load(rows) - twice(T.mean[rows, :])
        T.spread[rows, :] = row_mean(center * center)
    for _, _, _, rows in chunks():
        scale = lax.rsqrt(T.spread[rows, :] + epsilon)
        scales[rows, :] = scale.astype(bf16)
        store(rows, (load(rows) - twice(T.mean[rows, :])) * twice(scale))


def norm_back(gain, g, normed, scales, T, store):
    for _, _, _, rows in chunks():
        gn = g[rows, :] * gain
        T.mean[rows, :] = row_mean(gn)
        T.slope[rows, :] = row_mean(gn * normed[rows, :].astype(f32))
    for chunk in chunks():
        rows = chunk[3]
        gn = g[rows, :] * gain - twice(T.mean[rows, :])
        back = gn - normed[rows, :].astype(f32) * twice(T.slope[rows, :])
        store(chunk, twice(scales[rows, :].astype(f32)) * back)


def masked_pair(value, head):
    lane = lax.broadcasted_iota(jnp.int32, value.shape, 1)
    keep = (lane < 64) if head % 2 == 0 else (lane >= 64)
    return jnp.where(keep, value, jnp.zeros_like(value))


def pair_lanes(head):
    return slice(128 * (head // 2), 128 * (head // 2) + 128)


def two_heads(ref, p, rows):
    value = ref[rows, 128 * p : 128 * p + 128]
    return jnp.concatenate([masked_pair(value, 0), masked_pair(value, 1)], axis=0)


def column_of(t, side):
    return slice(256 * t + 128 * side, 256 * t + 128 * side + 128)


def stack_of(t):
    return slice(STACK[t], STACK[t] + TILES[t][1])


def of(member, start, stop):
    return slice(member * ROWS + start, member * ROWS + stop)


def chunks():
    for member in MEMBERS:
        for at, size in CHUNKS:
            yield member, at, size, pl.ds(member * ROWS + at, size)


def clear_tails(*refs):
    for ref in refs:
        for member in MEMBERS:
            rows = of(member, LIVE, ROWS)
            ref[rows, :] = jnp.zeros((ROWS - LIVE,) + ref.shape[1:], ref.dtype)


def forward_attend(x, lines, W, S, T):
    vec = W.vec

    def first(rows, n):
        S.n1[rows, :] = n.astype(bf16)
        T.a[rows, :] = (n * vec[:, 0:256] + vec[:, 256:512]).astype(bf16)

    normalize(lambda rows: x[rows, :].astype(f32), T, S.r1, first)
    clear_tails(S.n1)
    a = T.a[0:USED, :]
    packed = dot(a, W.inw[...])
    T.k[0:USED, :] = packed[:, 256:512].astype(bf16)
    S.q[0:USED, :] = (packed[:, 0:256] + vec[:, 512:768]).astype(bf16)
    S.v[0:USED, :] = (packed[:, 512:768] + vec[:, 768:1024]).astype(bf16)
    clear_tails(T.k, S.q, S.v)
    for member in MEMBERS:
        frames = lines[member]
        length = frames.shape[1]
        first = jnp.sum((frames == 0).astype(f32), axis=1, keepdims=True).astype(jnp.int32)
        last = jnp.minimum(first - 1 + WHOLE_FRAME * frames, length - 1)
        T.last[:, :] = jnp.full((1, ROWS), length - 1, jnp.int32)
        T.last[:, 0:length] = last
        for t, (at, stop, sure) in enumerate(TILES):
            keys = lax.broadcasted_iota(jnp.int32, (stop - sure, 128), 0) + sure
            seen = keys <= T.last[:, at : at + 128]
            T.mask[member, t, 0 : stop - sure, :] = jnp.where(seen, 0.0, masked_value)
    power = 0.125 * log2e
    units = [(p, member) for p in range(2) for member in MEMBERS]

    def scores(u):
        p, member = units[u]
        for t, (at, stop, _) in enumerate(TILES):
            T.s[u % 3, 0:stop, 256 * t : 256 * t + 256] = dot_upper(
                T.k[of(member, 0, stop), 128 * p : 128 * p + 128],
                two_heads(S.q, p, of(member, at, at + 128)),
            )

    def strips(u, t, side):
        _, stop, sure = TILES[t]
        for start in range(0, stop, 16):
            value = T.s[u % 3, start : start + 16, column_of(t, side)]
            if start >= sure:
                value = value + T.mask[units[u][1], t, start - sure : start - sure + 16, :]
            yield start, value

    columns = [(t, side) for t in range(3) for side in range(2)]

    def peaks(u):
        for t, side in columns:
            tops = [tree(jnp.maximum, eights(value)) for _, value in strips(u, t, side)]
            peak = jnp.max(tree(jnp.maximum, tops), axis=0, keepdims=True)
            T.peak[u % 3, :, column_of(t, side)] = peak * power

    def raises(u):
        for t, side in columns:
            lanes = column_of(t, side)
            peak = T.peak[u % 3, :, lanes]
            sums = []
            for start, value in strips(u, t, side):
                value = jnp.exp2(value * power - peak)
                T.s[u % 3, start : start + 16, lanes] = value
                sums.append(value[0:8] + value[8:16])
            total = jnp.sum(tree(jnp.add, sums), axis=0, keepdims=True)
            T.share[u % 3, :, lanes] = 1.0 / total

    def shares(u):
        p, member = units[u]
        for t, side in columns:
            lanes = column_of(t, side)
            share = T.share[u % 3, :, lanes]
            for start in range(0, TILES[t][1], 16):
                value = T.s[u % 3, start : start + 16, lanes] * share
                rows = slice(STACK[t] + start, STACK[t] + start + 16)
                S.pT[member, p, rows, 128 * side : 128 * side + 128] = value.astype(bf16)

    def mix(u):
        p, member = units[u]
        for t, (at, stop, _) in enumerate(TILES):
            both = dot(
                T.vT[128 * p : 128 * p + 128, of(member, 0, stop)],
                S.pT[member, p, stack_of(t), :],
            )
            for side in range(2):
                feats = slice(128 * p + 64 * side, 128 * p + 64 * side + 64)
                value = both[64 * side : 64 * side + 64, 128 * side : 128 * side + 128]
                S.mT[feats, of(member, at, at + 128)] = value.astype(bf16)

    scores(0)
    T.vT[...] = S.v[...].T
    peaks(0)
    scores(1)
    S.kT[...] = T.k[...].T
    raises(0)
    peaks(1)
    for u in range(len(units)):
        if u + 2 < len(units):
            scores(u + 2)
        shares(u)
        if u + 1 < len(units):
            raises(u + 1)
        if u + 2 < len(units):
            peaks(u + 2)
        mix(u)
    S.mT[256 : 256 + ONES, :] = jnp.ones((ONES, BOTH), bf16)
    mixed = S.mT[0:256, :].T
    T.f[...] = dot(mixed[0:USED], W.outw[...])
    for _, _, _, rows in chunks():
        S.middle[rows, :] = x[rows, :].astype(f32) + (T.f[rows, :] + vec[:, 1024:1280])

    def second(rows, n):
        S.n2[rows, :] = n.astype(bf16)
        S.second[rows, :] = (n * vec[:, 1280:1536] + vec[:, 1536:1792]).astype(bf16)

    normalize(lambda rows: S.middle[rows, :], T, S.r2, second)
    clear_tails(S.n2, S.second)


def forward_feed(W, S, T, out):
    vec = W.vec
    second = S.second[0:USED, :]

    T.g[...] = dot(second, W.upw[...])
    for c in range(4):
        cols = slice(256 * c, 256 * c + 256)
        for member, at, size, rows in chunks():
            bias = vec[:, 1792 + 256 * c : 2048 + 256 * c]
            act, slope = gelu_pair(T.g[rows, cols] + bias)
            S.act[rows, cols] = act.astype(bf16)
            S.dg[rows, cols] = slope.astype(bf16)
    clear_tails(S.act, S.dg)
    T.g[:, 0:256] = dot(S.act[0:USED, :], W.dnw[...])
    for member, at, size, rows in chunks():
        out(member, at, size, S.middle[rows, :] + (T.g[rows, 0:256] + vec[:, 2816:3072]))


def backward_feed(e_ref, W, S, T, acc):
    vec = W.vec
    e = e_ref[0:USED, :]
    eT = e_ref[...].T
    T.n2T[0:256, :] = S.n2[...].T

    T.g[...] = dot_upper(e, W.dnw[...])
    downs = dot(eT, S.act[...])
    for c in range(4):
        cols = slice(256 * c, 256 * c + 256)
        acc[4 + c, 0:256, :] += downs[:, cols]
        for member, at, size, rows in chunks():
            slope = S.dg[rows, cols].astype(f32)
            T.gr[rows, cols] = (T.g[rows, cols] * slope).astype(bf16)
    T.g[:, 0:256] = dot_upper(T.gr[0:USED, :], W.upw[...])
    ups = dot(T.n2T[...], T.gr[...])
    for c in range(4):
        acc[c] += ups[:, 256 * c : 256 * c + 256]
    columns = []

    def middle(chunk, back):
        rows = chunk[3]
        incoming = e_ref[rows, :].astype(f32)
        columns.append(tree(jnp.add, eights(incoming)))
        middle = incoming + back
        T.gmiddle[rows, :] = middle
        T.gp[rows, :] = middle.astype(bf16)

    norm_back(vec[:, 1280:1536], T.g.at[:, 0:256], S.n2, S.r2, T, middle)
    acc[4, 256 : 256 + ONES, :] += jnp.sum(tree(jnp.add, columns), axis=0, keepdims=True)


def backward_attend(W, S, T, acc, out):
    vec = W.vec
    gp = T.gp[...]
    T.gm[0:USED, :] = dot_upper(gp[0:USED], W.outw[...]).astype(bf16)
    T.n1T[0:256, :] = S.n1[...].T
    gmT = dot_upper(W.outw[...], gp)
    for h in range(HEADS):
        feats = slice(64 * h, 64 * h + 64)
        product = gmT[feats] * S.mT[feats, :].astype(f32)
        T.inner[h : h + 1, :] = jnp.sum(product, axis=0, keepdims=True)
    units = [(p, member) for p in range(2) for member in MEMBERS]

    def slopes(u):
        p, member = units[u]
        for t, (at, stop, _) in enumerate(TILES):
            queries = of(member, at, at + 128)
            gprobs = dot_upper(
                S.v[of(member, 0, stop), 128 * p : 128 * p + 128], two_heads(T.gm, p, queries)
            )
            probs = S.pT[member, p, stack_of(t), :].astype(f32)
            inner = [T.inner[2 * p + side : 2 * p + side + 1, queries] for side in range(2)]
            slope = probs * (gprobs - jnp.concatenate(inner, axis=1))
            T.ds[u % 2, stack_of(t), :] = slope.astype(bf16)

    def gather(parts, scale=None):
        start = 0
        for t, (_, stop, _) in enumerate(TILES):
            value = tree(jnp.add, [part[start:stop] for part in parts[t:]])
            value = value if scale is None else value * scale
            yield start, stop, value.astype(bf16)
            start = stop

    def products(u):
        p, member = units[u]
        gk, gv = [], []
        for t, (at, stop, _) in enumerate(TILES):
            queries = of(member, at, at + 128)
            ds = T.ds[u % 2, stack_of(t), :]
            gk.append(dot(ds, two_heads(S.q, p, queries)))
            gv.append(dot(S.pT[member, p, stack_of(t), :], two_heads(T.gm, p, queries)))
            both = dot(S.kT[128 * p : 128 * p + 128, of(member, 0, stop)], ds) * 0.125
            for side in range(2):
                feats = slice(128 * p + 64 * side, 128 * p + 64 * side + 64)
                value = both[64 * side : 64 * side + 64, 128 * side : 128 * side + 128]
                T.gqT[feats, queries] = value.astype(bf16)
        for start, stop, value in gather(gk, 0.125):
            T.gqkv[of(member, start, stop), 256 + 128 * p : 384 + 128 * p] = value
        for start, stop, value in gather(gv):
            T.gqkv[of(member, start, stop), 512 + 128 * p : 640 + 128 * p] = value

    slopes(0)
    acc[3] += dot(S.mT[...], gp)
    for u in range(len(units)):
        if u + 1 < len(units):
            slopes(u + 1)
        products(u)
    T.gqkv[:, 0:256] = T.gqT[...].T
    T.g[:, 0:256] = dot_upper(T.gqkv[0:USED, :], W.inw[...])
    ins = dot(T.n1T[...], T.gqkv[...])
    for b in range(3):
        acc[b] += ins[:, 256 * b : 256 * b + 256]

    def finish(chunk, back):
        member, at, size, rows = chunk
        out(member, at, size, T.gmiddle[rows, :] + back)

    norm_back(vec[:, 0:256], T.g.at[:, 0:256], S.n1, S.r1, T, finish)


ATTEND_SAVED = dict(
    n1=((BOTH, 256), bf16, 0),
    r1=((BOTH, 128), bf16, 0),
    v=((BOTH, 256), bf16, 0),
    kT=((256, BOTH), bf16, 1),
    q=((BOTH, 256), bf16, 0),
    pT=((PAIR, 2, STACKED, 256), bf16, 0),
    mT=((256 + ONES, BOTH), bf16, 1),
    n2=((BOTH, 256), bf16, 0),
    r2=((BOTH, 128), bf16, 0),
)
BETWEEN = dict(second=((BOTH, 256), bf16, 0), middle=((BOTH, 256), f32, 0))
GELU_SAVED = dict(act=((BOTH, 1024), bf16, 0), dg=((BOTH, 1024), bf16, 0))
ATTEND_SCRATCH = dict(
    a=((BOTH, 256), bf16, 0),
    k=((BOTH, 256), bf16, 0),
    vT=((256, BOTH), bf16, 1),
    last=((1, ROWS), jnp.int32, 0),
    mask=((PAIR, 3, 144, 128), f32, 0),
    s=((3, LIVE, 2 * ROWS), f32, 0),
    peak=((3, 1, 2 * ROWS), f32, 0),
    share=((3, 1, 2 * ROWS), f32, 0),
    mean=((BOTH, 128), f32, 0),
    spread=((BOTH, 128), f32, 0),
    f=((USED, 256), f32, 0),
    x=((BOTH, 256), bf16, 0),
)
BACK_SCRATCH = dict(
    mean=((BOTH, 128), f32, 0),
    slope=((BOTH, 128), f32, 0),
    g=((USED, 1024), f32, 0),
    gr=((BOTH, 1024), bf16, 0),
    gp=((BOTH, 256), bf16, 0),
    gmiddle=((BOTH, 256), f32, 0),
    n1T=((256 + ONES, BOTH), bf16, 1),
    n2T=((256 + ONES, BOTH), bf16, 1),
    gm=((BOTH, 256), bf16, 0),
    inner=((8, BOTH), f32, 0),
    ds=((2, STACKED, 256), bf16, 0),
    gqT=((256, BOTH), bf16, 0),
    gqkv=((BOTH, 768), bf16, 0),
)
ATTEND_WEIGHTS = dict(
    vec=((1, 3072), f32, 0),
    inw=((256, 768), bf16, 0),
    outw=((256, 256), bf16, 0),
)
WEIGHTS = dict(
    upw=((256, 1024), bf16, 0),
    dnw=((1024, 256), bf16, 0),
)
FEED_WEIGHTS = dict(WEIGHTS, vec=ATTEND_WEIGHTS["vec"])
WEIGHTS = dict(ATTEND_WEIGHTS, **WEIGHTS)
ACC = dict(
    feed=((8, 256 + ONES, 256), f32, 0),
    attend=((4, 256 + ONES, 256), f32, 0),
)
FEED_HALF = 8 * 256 + 128
ATTEND_HALF = 4 * 256 + 128
WIRE = FEED_HALF + ATTEND_HALF
VMEM_LIMIT = 62 * 1024 * 1024


def load_padded(ref, member, source, length):
    whole = length // 16 * 16
    ref[of(member, whole, ROWS), :] = jnp.zeros((ROWS - whole, 256), bf16)
    ref[of(member, 0, length), :] = source[...]


def fetch_weights(refs, layer, place, attend, feed=None, meanwhile=None):
    vec, inw, outw = attend
    core = place[2]

    def run(pairs):
        copies = [
            pltpu.make_async_copy(source, target, refs.sem.at[i])
            for i, (source, target) in enumerate(pairs)
        ]
        for copy in copies:
            copy.start()
        if meanwhile is not None:
            meanwhile()
        for copy in copies:
            copy.wait()

    @pl.when(place[1] == layer)
    def _():
        pairs = [(refs.own[0], vec)]
        if inw is not None:
            pairs += [(refs.own[1], inw), (refs.own[2], outw)]
        if feed is not None:
            pairs += list(zip(refs.own[3:], feed))
        run(pairs)

    @pl.when(place[1] != layer)
    def _():
        pairs = [(refs.far[0].at[128:144, :], refs.bits)]
        if inw is not None:
            for i in range(2):
                at = (core if i == 0 else 1 - core) * 128
                rows = pl.ds(pl.multiple_of(at, 128), 128)
                pairs.append((refs.far[i].at[0:128, 0:768], inw.at[rows, :]))
                pairs.append((refs.far[i].at[0:128, 768:1024], outw.at[rows, :]))
        if feed is not None:
            upw, dnw = feed
            for i in range(2):
                part = refs.far[2 + i]
                at = core if i == 0 else 1 - core
                rows = pl.ds(pl.multiple_of(at * 128, 128), 128)
                pairs.append((part.at[0:128, :], upw.at[rows, :]))
                for j in range(4):
                    rows = pl.ds(pl.multiple_of(at * 512 + 128 * j, 128), 128)
                    lanes = slice(256 * j, 256 * j + 256)
                    pairs.append((part.at[128:256, lanes], dnw.at[rows, :]))
        run(pairs)
        parts = refs.bits[...].astype(f32)
        for j in range(3):
            value = parts[j : j + 1] + parts[3 + j : 4 + j] + parts[6 + j : 7 + j]
            vec[:, 1024 * j : 1024 * j + 1024] = value


def emit_rows(target, at, blocks):
    tail = at + 512 * len(blocks)
    target[tail : tail + 128, :] = jnp.zeros((128, 128), target.dtype)
    for j, block in enumerate(blocks):
        for side in range(2):
            lanes = slice(128 * side, 128 * side + 128)
            part = 2 * j + side
            target[at + 256 * part : at + 256 * part + 256, :] = block[0:256, lanes].astype(
                target.dtype
            )
            target[tail + ONES * part : tail + ONES * part + ONES, :] = block[
                256 : 256 + ONES, lanes
            ].astype(target.dtype)


def emit_half(target, at, half, acc):
    emit_rows(target, at, [acc.feed.at[4 * half + b] for b in range(4)])
    emit_rows(target, at + FEED_HALF, [acc.attend.at[2 * half + b] for b in range(2)])


def emit_halves(refs, core):
    for half in range(2):

        @pl.when(core == half)
        def _(half=half):
            emit_half(refs.keep, 0, half, refs)
            emit_half(refs.send, 0, 1 - half, refs)


def pack_kernel(place, *refs):
    vec, half = refs[-2:]
    inw, outw = refs[8:10]
    at = 0
    for ref in refs[:8]:
        vec[:, at : at + ref.shape[1]] = ref[...]
        at += ref.shape[1]
    rows = pl.ds(pl.multiple_of(place[2] * 128, 128), 128)
    half[0:128, 0:768] = inw[0, rows, :]
    half[0:128, 768:1024] = outw[0, rows, :]
    rest = jnp.concatenate([vec[:, 1024 * j : 1024 * j + 1024] for j in range(3)], axis=0)
    parts = []
    for _ in range(3):
        part = rest.astype(bf16).astype(f32)
        parts.append(part)
        rest = rest - part
    parts.append(jnp.zeros((7, 1024), f32))
    half[128:144, :] = jnp.concatenate(parts, axis=0).astype(bf16)


def pack_feed_kernel(place, upw, dnw, half):
    half[0:128, :] = upw[0, pl.ds(pl.multiple_of(place[2] * 128, 128), 128), :]
    for j in range(4):
        rows = pl.ds(pl.multiple_of(place[2] * 512 + 128 * j, 128), 128)
        half[128:256, 256 * j : 256 * j + 256] = dnw[0, rows, :]


def zero(refs):
    for ref in refs:
        ref[...] = jnp.zeros(ref.shape, ref.dtype)


def set_ones(*refs):
    for ref in refs:
        ref[256 : 256 + ONES, :] = jnp.ones((ONES, BOTH), bf16)


def attend_kernel(place, refs):
    step = pl.program_id(0)

    @pl.when(step == 0)
    def _():
        fetch_weights(refs, 0, place, (refs.vec, refs.inw, refs.outw))

    length = refs.frames.shape[1]
    lines = []
    for member in MEMBERS:
        load_padded(refs.x, member, refs.tokens.at[member], length)
        lines.append(refs.frames[pl.ds(place[0] + PAIR * step + member, 1), :])
    forward_attend(refs.x, lines, refs, refs, refs)


def middle_kernel(place, refs):
    step = pl.program_id(0)

    @pl.when(step == 0)
    def _():
        def clear():
            zero([refs.feed, refs.attend])
            clear_tails(refs.gqkv, refs.gr, refs.gp, refs.gm, refs.x, refs.low_second)
            set_ones(refs.n1T, refs.n2T)

        held = (refs.low_vec, None, None)
        fetch_weights(refs, 0, place, held, (refs.low_upw, refs.low_dnw), clear)
        held = (refs.vec, refs.inw, refs.outw)
        fetch_weights(refs, 1, place, held, (refs.upw, refs.dnw))

    length = refs.frames.shape[1]
    upper = place[1] > 0
    lower = SimpleNamespace(upw=refs.low_upw, dnw=refs.low_dnw, vec=refs.low_vec)
    below = SimpleNamespace(
        second=refs.low_second, middle=refs.low_middle, act=refs.low_act, dg=refs.low_dg
    )

    def out_lower(member, at, size, rows):
        refs.x[of(member, at, at + size), :] = rows.astype(bf16)

    def out(member, at, size, rows):
        size = min(size, length - at)
        rows = rows[:size].astype(bf16)
        low, high = rows[:, 0:128], rows[:, 128:256]
        refs.mine[member, at : at + size, :] = jnp.where(upper, high, low)
        refs.other[member, at : at + size, :] = jnp.where(upper, low, high)

    def out_back(member, at, size, rows):
        refs.e0[of(member, at, at + size), :] = rows.astype(bf16)

    lines = []
    for member in MEMBERS:
        load_padded(refs.e, member, refs.cotangent.at[member], length)
        lines.append(refs.frames[pl.ds(place[0] + PAIR * step + member, 1), :])
    for member, at, size, rows in chunks():
        n = refs.low_n2[rows, :].astype(f32)
        second = n * refs.low_vec[:, 1280:1536] + refs.low_vec[:, 1536:1792]
        refs.low_second[rows, :] = second.astype(bf16)
    forward_feed(lower, below, refs, out_lower)
    forward_attend(refs.x, lines, refs, refs, refs)
    forward_feed(refs, refs, refs, out)
    backward_feed(refs.e, refs, refs, refs, refs.feed)
    clear_tails(refs.e0)
    backward_attend(refs, refs, refs, refs.attend, out_back)

    @pl.when(step == pl.num_programs(0) - 1)
    def _():
        emit_halves(refs, place[2])


DEFERRED = ("v", "kT", "q", "pT", "mT", "n1", "r1")


def back_kernel(place, refs):
    step = pl.program_id(0)

    @pl.when(step == 0)
    def _():
        def clear():
            zero([refs.feed, refs.attend])
            clear_tails(refs.gqkv, refs.gr, refs.gp, refs.gm)
            set_ones(refs.n1T, refs.n2T)

        held = (refs.vec, refs.inw, refs.outw)
        fetch_weights(refs, 0, place, held, (refs.upw, refs.dnw), clear)

    length = refs.mine.shape[1]
    upper = place[1] > 0

    def out(member, at, size, rows):
        size = min(size, length - at)
        low, high = rows[:size, 0:128], rows[:size, 128:256]
        refs.mine[member, at : at + size, :] = jnp.where(upper, high, low)
        refs.other[member, at : at + size, :] = jnp.where(upper, low, high).astype(bf16)

    def fetches(at_step):
        slot = at_step % 2
        for i, name in enumerate(DEFERRED):
            shape, _, axis = ATTEND_SAVED[name]
            at = at_step * shape[axis]
            if shape[axis] > PAIR:
                at = pl.multiple_of(at, 128)
            where = [slice(None)] * len(shape)
            where[axis] = pl.ds(at, shape[axis])
            source = getattr(refs, "whole_" + name).at[tuple(where)]
            target = getattr(refs, name).at[slot]
            yield pltpu.make_async_copy(source, target, refs.sem.at[7 * slot + i])

    @pl.when(step == 0)
    def _():
        for copy in fetches(step):
            copy.start()

    backward_feed(refs.e0, refs, refs, refs, refs.feed)
    for copy in fetches(step):
        copy.wait()

    @pl.when(step < pl.num_programs(0) - 1)
    def _():
        for copy in fetches(step + 1):
            copy.start()

    held = {name: getattr(refs, name).at[step % 2] for name in DEFERRED}
    backward_attend(refs, SimpleNamespace(**held), refs, refs.attend, out)
    last = step == pl.num_programs(0) - 1

    @pl.when(jnp.logical_not(last))
    def _():
        refs.early[...] = refs.other[...]

    @pl.when(last)
    def _():
        refs.late[...] = refs.other[...]

    @pl.when(step == pl.num_programs(0) - 1)
    def _():
        emit_halves(refs, place[2])


def column(row):
    return jnp.broadcast_to(row, (8, 256)).T[:, 0:1]


def line(value):
    return jnp.broadcast_to(value, (256, 128)).T[0:1]


def finish(halves, inw, upw, again, ashift, mgain, mshift, outs):
    ga, sa, giw, gib, gow, gob, gm, sm, guw, gub, gdw, gdb = outs

    def block(half, at, count, part):
        start, tail = at + 256 * part, at + 512 * count + ONES * part
        rows = halves[half][start : start + 256, :].astype(f32)
        return rows, halves[half][tail : tail + ONES, :].astype(f32)[0:1]

    gain, shift = column(mgain[...]), column(mshift[...])
    of_gain, of_shift = [], []
    for part in range(8):
        rows, sums = block(0, 0, 4, part)
        lanes = slice(128 * part, 128 * part + 128)
        guw[0, :, lanes] = gain * rows + shift * sums
        gub[:, lanes] = sums
        weight = upw[0, :, lanes].astype(f32)
        of_gain.append(weight * rows)
        of_shift.append(weight * sums)
    gm[...] = line(jnp.sum(tree(jnp.add, of_gain), axis=1, keepdims=True))
    sm[...] = line(jnp.sum(tree(jnp.add, of_shift), axis=1, keepdims=True))
    for part in range(8):
        rows, sums = block(1, 0, 4, part)
        gdw[0, 128 * part : 128 * part + 128, :] = rows.T
        if part < 2:
            gdb[:, 128 * part : 128 * part + 128] = sums
    gain, shift = column(again[...]), column(ashift[...])
    of_gain, of_shift = [], []
    for part in range(8):
        rows, sums = block(part // 4, FEED_HALF, 2, part % 4)
        if part < 6:
            lanes = slice(128 * part, 128 * part + 128)
            giw[0, :, lanes] = gain * rows + shift * sums
            weight = inw[0, :, lanes].astype(f32)
            of_gain.append(weight * rows)
            of_shift.append(weight * sums)
            if part < 2:
                gib[:, lanes] = sums
            elif part >= 4:
                gib[:, 128 * part - 256 : 128 * part - 128] = sums
        else:
            lanes = slice(128 * (part - 6), 128 * (part - 6) + 128)
            gow[0, :, lanes] = rows
            gob[:, lanes] = sums
    ga[...] = line(jnp.sum(tree(jnp.add, of_gain), axis=1, keepdims=True))
    sa[...] = line(jnp.sum(tree(jnp.add, of_shift), axis=1, keepdims=True))


def final_kernel(place, own, far, *refs):
    weights, outs = refs[:6], refs[6:]

    @pl.when(place[2] == 0)
    def _():
        finish((own, far), *weights, outs)

    @pl.when(place[2] != 0)
    def _():
        finish((far, own), *weights, outs)


SMEM = pl.BlockSpec(memory_space=pltpu.SMEM)
VMEM = pl.BlockSpec(memory_space=pltpu.VMEM)
ANY = pl.BlockSpec(memory_space=pl.ANY)


def step_spec(shape, axis=0, held=False):
    def index(i, place):
        at = i + place[0] // PAIR if held else i
        return tuple(at if d == axis else 0 for d in range(len(shape)))

    return pl.BlockSpec(shape, index)


def constant(shape):
    return pl.BlockSpec(shape, lambda i, place: (0,) * len(shape))


def step_arrays(table, steps):
    return {
        name: (
            step_spec(shape, axis),
            jax.ShapeDtypeStruct(
                tuple(n * steps if d == axis else n for d, n in enumerate(shape)), kind
            ),
        )
        for name, (shape, kind, axis) in table.items()
    }


def call(kernel, steps, place, own, far, inputs, outputs, scratch, cost):
    own, far = list(own), list(far)
    count, other = len(own), len(far)
    scratch = dict(scratch, bits=((16, 1024), bf16, 0))
    names = list(inputs) + list(outputs) + list(scratch)

    def run(place, *refs):
        rest = refs[count + other :]
        named = SimpleNamespace(**dict(zip(names, rest)))
        named.own, named.far, named.sem = refs[:count], refs[count : count + other], rest[-1]
        kernel(place, named)

    results = pl.pallas_call(
        run,
        grid_spec=pltpu.PrefetchScalarGridSpec(
            num_scalar_prefetch=1,
            grid=(steps,),
            in_specs=[ANY] * (count + other) + [spec for spec, _ in inputs.values()],
            out_specs=[spec for spec, _ in outputs.values()],
            scratch_shapes=[pltpu.VMEM(shape, kind) for shape, kind, _ in scratch.values()]
            + [pltpu.SemaphoreType.DMA((16,))],
        ),
        out_shape=[shape for _, shape in outputs.values()],
        compiler_params=pltpu.CompilerParams(
            vmem_limit_bytes=VMEM_LIMIT, dimension_semantics=("arbitrary",)
        ),
        cost_estimate=pl.CostEstimate(flops=cost, bytes_accessed=3000000, transcendentals=0),
    )(place, *own, *far, *(operand for _, operand in inputs.values()))
    return dict(zip(outputs, results))


def body(
    tokens,
    cotangent,
    frame_ids,
    attend_gain,
    attend_shift,
    inward_weight,
    inward_bias,
    outward_weight,
    outward_bias,
    mixing_gain,
    mixing_shift,
    up_weight,
    up_bias,
    down_weight,
    down_bias,
):
    section = lax.axis_index("section")
    batch = lax.axis_index("batch")
    batches = lax.axis_size("batch")
    sequences, length, width = tokens.shape
    half = sequences // 2
    steps = half // PAIR
    place = jnp.stack([section * half, section, batch % 2]).astype(jnp.int32)

    def mine(value):
        return lax.dynamic_slice_in_dim(value, section * half, half, 0)

    def across(value):
        return lax.ppermute(value, "section", ((0, 1), (1, 0)))

    def between_cores(value):
        return lax.ppermute(value, "batch", [(b, b ^ 1) for b in range(batches)])

    everyone = ("section", "batch")
    beyond = [1 << bit for bit in range(3, batches.bit_length() - 1)]
    cubes = [
        [s * batches + base + c + 2 * i for s in range(2) for i in range(4)]
        for base in range(0, batches, 8)
        for c in range(2)
    ]

    def exchange(value):
        return lax.all_to_all(value, everyone, 0, 0, tiled=True, axis_index_groups=cubes)

    def partner(value, flip):
        return lax.ppermute(value, "batch", [(b, b ^ flip) for b in range(batches)])

    vectors, half_weights = pl.pallas_call(
        pack_kernel,
        in_specs=[SMEM] + [VMEM] * 10,
        out_specs=[VMEM] * 2,
        out_shape=[
            jax.ShapeDtypeStruct((1, 3072), f32),
            jax.ShapeDtypeStruct((144, 1024), bf16),
        ],
    )(
        place,
        attend_gain,
        attend_shift,
        inward_bias,
        outward_bias,
        mixing_gain,
        mixing_shift,
        up_bias,
        down_bias,
        inward_weight,
        outward_weight,
    )
    own_attend = (vectors, inward_weight[0], outward_weight[0])
    half_feed = pl.pallas_call(
        pack_feed_kernel,
        in_specs=[SMEM] + [VMEM] * 2,
        out_specs=VMEM,
        out_shape=jax.ShapeDtypeStruct((256, 1024), bf16),
    )(place, up_weight, down_weight)
    arrived, half_feed, held_tokens, held_cotangent = lax.optimization_barrier(
        (across(half_weights), half_feed, mine(tokens), mine(cotangent))
    )
    far_attend = (arrived, between_cores(arrived))
    arrived_feed = across(half_feed)

    def whole_frames():
        return constant((sequences, length)), frame_ids

    table = dict(ATTEND_SAVED)
    table.update(middle=BETWEEN["middle"])
    scratch = dict(ATTEND_SCRATCH)
    scratch.update(ATTEND_WEIGHTS)
    scratch.update(second=BETWEEN["second"])
    kept = call(
        attend_kernel,
        steps,
        place,
        own_attend,
        far_attend,
        dict(tokens=(step_spec((PAIR, length, 256)), held_tokens), frames=whole_frames()),
        step_arrays(table, steps),
        scratch,
        18000000000,
    )

    own = [*own_attend, up_weight[0], down_weight[0]]
    arrived_feed, kept["n2"] = lax.optimization_barrier((arrived_feed, kept["n2"]))
    far = [*far_attend, arrived_feed, between_cores(arrived_feed)]

    scratch = {}
    for table in (ATTEND_SCRATCH, BACK_SCRATCH, ATTEND_SAVED, BETWEEN, GELU_SAVED, WEIGHTS, ACC):
        scratch.update(table)
    for name in FEED_WEIGHTS:
        scratch["low_" + name] = WEIGHTS[name]
    scratch.update(e=((BOTH, 256), bf16, 0), low_second=((BOTH, 256), bf16, 0))
    outputs = {"low_" + name: pair for name, pair in step_arrays(GELU_SAVED, steps).items()}
    outputs.update(step_arrays(dict(e0=((BOTH, 256), bf16, 0)), steps))
    outputs.update(
        mine=(
            step_spec((PAIR, length, 128), 0, True),
            jax.ShapeDtypeStruct((sequences, length, 128), bf16),
        ),
        other=(
            step_spec((PAIR, length, 128)),
            jax.ShapeDtypeStruct((half, length, 128), bf16),
        ),
        keep=(constant((WIRE, 128)), jax.ShapeDtypeStruct((WIRE, 128), bf16)),
        send=(constant((WIRE, 128)), jax.ShapeDtypeStruct((WIRE, 128), bf16)),
    )
    results = call(
        middle_kernel,
        steps,
        place,
        own,
        far,
        dict(
            low_n2=(step_spec((BOTH, 256)), kept["n2"]),
            low_middle=(step_spec((BOTH, 256)), kept["middle"]),
            cotangent=(step_spec((PAIR, length, 256)), held_cotangent),
            frames=whole_frames(),
        ),
        outputs,
        scratch,
        72000000000,
    )
    kept.update(act=results["low_act"], dg=results["low_dg"])
    out_own = results["mine"]

    chunk = WIRE // 8

    def sum_cores(keep, send):
        total = keep.astype(f32) + between_cores(send).astype(f32)
        return total.astype(bf16).reshape(8, chunk, 128)

    def chunk_of(parts):
        total = jnp.sum(parts.astype(f32), axis=0).astype(bf16)
        for flip in beyond:
            total = lax.optimization_barrier(total)
            total = (total.astype(f32) + partner(total, flip).astype(f32)).astype(bf16)
        return total

    upper_parts, e0 = lax.optimization_barrier(
        (sum_cores(results["keep"], results["send"]), results["e0"])
    )
    upper_parts = exchange(upper_parts)
    out_arrived = across(results["other"])

    table = dict(ATTEND_SAVED)
    table.update(GELU_SAVED)
    inputs = {
        name: (spec, kept[name]) for name, (spec, _) in step_arrays(table, steps).items()
    }
    inputs.update(e0=(step_spec((BOTH, 256)), e0))
    for name in DEFERRED:
        inputs["whole_" + name] = (ANY, inputs.pop(name)[1])
    scratch = dict(BACK_SCRATCH)
    scratch.update(WEIGHTS)
    scratch.update(ACC)
    scratch.update(
        {name: ((2,) + ATTEND_SAVED[name][0], bf16, 0) for name in DEFERRED}
    )
    scratch.update(other=((PAIR, length, 128), bf16, 0))
    results = call(
        back_kernel,
        steps,
        place,
        own,
        far,
        inputs,
        dict(
            mine=(
                step_spec((PAIR, length, 128), 0, True),
                jax.ShapeDtypeStruct((sequences, length, 128), f32),
            ),
            early=(
                pl.BlockSpec((PAIR, length, 128), lambda i, p: (jnp.minimum(i, steps - 2), 0, 0)),
                jax.ShapeDtypeStruct((half - PAIR, length, 128), bf16),
            ),
            late=(
                constant((PAIR, length, 128)),
                jax.ShapeDtypeStruct((PAIR, length, 128), bf16),
            ),
            keep=(constant((WIRE, 128)), jax.ShapeDtypeStruct((WIRE, 128), bf16)),
            send=(constant((WIRE, 128)), jax.ShapeDtypeStruct((WIRE, 128), bf16)),
        ),
        scratch,
        40000000000,
    )
    upper_parts, out_arrived, grad_own, grad_early, grad_late, keep, send = (
        lax.optimization_barrier(
            (
                upper_parts,
                out_arrived,
                results["mine"],
                results["early"],
                results["late"],
                results["keep"],
                results["send"],
            )
        )
    )
    late_arrived = across(grad_late)
    lower_parts, late_arrived = lax.optimization_barrier((sum_cores(keep, send), late_arrived))
    lower_parts = exchange(lower_parts)
    early_arrived = across(grad_early)
    upper_chunk = chunk_of(upper_parts)

    ours = (jnp.arange(sequences) // half == section)[None, :, None]

    def assemble(held, arrived):
        arrived = jnp.concatenate([arrived, arrived], axis=0).astype(held.dtype)
        value = jnp.where(ours, held.transpose(1, 0, 2), arrived.transpose(1, 0, 2))
        return with_layout_constraint(value, Layout((0, 1, 2)))

    layer_out = assemble(out_own, out_arrived)
    lower_chunk, layer_out, early_arrived = lax.optimization_barrier(
        (chunk_of(lower_parts), layer_out, early_arrived)
    )
    spread = (4, chunk, 128)
    own_half = exchange(
        jnp.concatenate(
            [jnp.broadcast_to(lower_chunk, spread), jnp.broadcast_to(upper_chunk, spread)]
        )
    )
    input_grad = assemble(grad_own, jnp.concatenate([early_arrived, late_arrived], axis=0))
    own_half, input_grad = lax.optimization_barrier((own_half, input_grad))
    far_half = between_cores(own_half)

    grads = (
        (1, 256),
        (1, 256),
        (1, 256, 768),
        (1, 512),
        (1, 256, 256),
        (1, 256),
        (1, 256),
        (1, 256),
        (1, 256, 1024),
        (1, 1024),
        (1, 1024, 256),
        (1, 256),
    )
    finals = pl.pallas_call(
        final_kernel,
        in_specs=[SMEM] + [VMEM] * 8,
        out_specs=[VMEM] * 12,
        out_shape=[jax.ShapeDtypeStruct(shape, f32) for shape in grads],
        compiler_params=pltpu.CompilerParams(vmem_limit_bytes=VMEM_LIMIT),
    )(
        place,
        own_half.reshape(WIRE, 128),
        far_half.reshape(WIRE, 128),
        inward_weight,
        up_weight,
        attend_gain,
        attend_shift,
        mixing_gain,
        mixing_shift,
    )
    return (layer_out.transpose(1, 0, 2), input_grad.transpose(1, 0, 2), *finals)


def solution(mesh):
    spread = P("section", None)
    deep = P("section", None, None)
    weights = (
        spread,
        spread,
        deep,
        spread,
        deep,
        spread,
        spread,
        spread,
        deep,
        spread,
        deep,
        spread,
    )
    rows = P("batch", None, None)
    return jax.shard_map(
        body,
        mesh=mesh,
        in_specs=(rows, rows, P("batch", None)) + weights,
        out_specs=(P("batch", None, "section"),) * 2 + weights,
        check_vma=False,
    )
```

time: 1220 us -> 188 us (0.15); the launches traced: 1210 us -> 187 us
  matrix products: 487 us -> 0 us
  local copies, waits for them, and re-layouts: 423 us -> 10.7 us
  other arithmetic: 129 us -> 13 us
  Pallas kernels: 0 us -> 105 us
  blocking collectives: 58.7 us -> 0 us
  waiting for transfers between devices: 67.6 us -> 29.7 us
  between operations: 17.6 us -> 0.8 us
    dot_general x150 -> x0, matrix products: 444 us -> none  [the longest x30 201 us: matmul(): return jnp.dot(left, right, preferred_element_type=jnp.float32)]
    reshape x33 -> x0, local copies, waits for them, and re-layouts: 136 us -> none  [the longest x10 52.9 us: layer_forward(): packed.reshape(sequences // 2, 2, length, 3, HEADS, width // HEADS)]
    while x136 -> x0, local copies, waits for them, and re-layouts: 136 us -> none  [the longest x10 69.2 us: layer_forward(): lax.map(lambda item: attend_group(item[0], item[1]), (grouped, frames.res...]
    pallas_call x0 -> x6, Pallas kernels: none -> 105 us  [the longest x3 96.5 us: call(): pl.pallas_call(run, grid_spec=pltpu.PrefetchScalarGridSpec(num_scalar_pre...]
    reduce_sum x60 -> x2, other arithmetic: 75.4 us -> 0.24 us  [chunk_of(): total = jnp.sum(parts.astype(f32), axis=0).astype(bf16)]
    psum x1 -> x0, blocking collectives: 58.7 us -> none  [body(): totals = lax.psum(totals, 'batch')]
    sub x10 -> x0, matrix products: 43.5 us -> none  [attend_group(): weights = jnp.exp(scores - peak)]
    concatenate x2 -> x0, local copies, waits for them, and re-layouts: 35.8 us -> none  [the longest x1 18.5 us: body(): grad_all = jnp.concatenate(grad_ticks[1:], axis=0)]
  transfers between devices with their start and end apart: 10 -> 15, of which waited for: 5 -> 8; matrix products, arithmetic and copies ran while one was open for 12% -> 10% of each run, Pallas kernels for 0% -> 25%
where the time goes in v1:
time: 188 us; the launch traced here: 187 us
  Pallas kernels  105 us (56%)
  waiting for transfers between devices  29.7 us (16%)
  starting transfers between devices  27.7 us (15%)
  other arithmetic  13 us (7%)
  local copies, waits for them, and re-layouts  10.7 us (6%)
    pallas_call x3, Pallas kernels, call(): pl.pallas_call(run, grid_spec=pltpu.PrefetchScalarGridSpec(num_scalar_pre...  96.5 us
    all_to_all x3, waiting for transfers between devices, exchange(): lax.all_to_all(value, everyone, 0, 0, tiled=True, axis_index_groups=cubes)  16.2 us
    all_to_all x3, starting transfers between devices, exchange(): lax.all_to_all(value, everyone, 0, 0, tiled=True, axis_index_groups=cubes)  12.6 us
    ppermute x5, starting transfers between devices, across(): return lax.ppermute(value, 'section', ((0, 1), (1, 0)))  10.2 us
    select_n x2, other arithmetic, assemble(): value = jnp.where(ours, held.transpose(1, 0, 2), arrived.transpose(1, 0, 2))  7.76 us
    ppermute x5, waiting for transfers between devices, across(): return lax.ppermute(value, 'section', ((0, 1), (1, 0)))  4.84 us
    pallas_call x1, Pallas kernels, body(): pl.pallas_call(final_kernel, in_specs=[SMEM] + [VMEM] * 8, out_specs=[VME...  4.67 us
    ppermute x2, waiting for transfers between devices, partner(): return lax.ppermute(value, 'batch', [(b, b ^ flip) for b in range(batches)])  4.6 us
  transfers between devices with their start and end apart: 15, of which 8 were waited for; matrix products, arithmetic and copies ran while one was open for 10% of the time, Pallas kernels for 25%

profile of v1, /device:TPU:0, one launch (start us, length us, event | category | flops | bytes accessed | tf_op | source)
XLA Modules:
  0.0 187.0 jit_solution(13876745310738150047)
XLA Ops:
  0.7 0.6 pad_add_fusion.place
  1.2 1.9 %shard_map.254 = (f32[1,3072]{1,0:T(1,128)}, bf16[144,1024]{1,0:T(8,128)(2,1)}) custom-call(s32[3]{0:T(128)} %pad_add_fusion.place, f32[1,256]{1,0:T(1,128)} %refs_2_.3, f32[1,256]{1,0:T(1,128)} %refs_3_.3, f32[1,512]{1,0:T(1,128)} %refs_2_.2, f32[1,256]{1,0:T(1,128)} %refs_3_.2, f32[1,256]{1,0:T(1,128)} %refs_4_.3, f32[1,256]{1,0:T(1,128)} %refs_5_.3, ...), custom_call_target="tpu_custom_call" | custom-call | tf_op jit(solution)/shard_map/pallas_call | solution.py:872
  3.2 2.9 %collective-permute-start = (bf16[144,1024]{1,0:T(8,128)(2,1)}, bf16[144,1024]{1,0:T(8,128)(2,1)S(1)}, u32[]{:S(2)}, u32[]{:S(2)}) collective-permute-start(bf16[144,1024]{1,0:T(8,128)(2,1)} %get-tuple-element.73), channel_id=1, source_target_pairs={{0,16},{16,0},{1,17},{17,1},{2,18},{18,2},{3,19},{19,3},{4,20},{20... | collective-permute-start | bytes 884744 | tf_op jit(solution)/shard_map/ppermute | solution.py:853
  6.1 2.0 %constant_dynamic-slice_fusion = (bf16[8,357,256]{2,0,1:T(8,128)(2,1)S(1)}, bf16[8,357,256]{2,0,1:T(8,128)(2,1)S(1)}) fusion(bf16[16,357,256]{2,0,1:T(8,128)(2,1)} %param.16, s32[]{:T(128)S(6)} %select_n.35, bf16[16,357,256]{2,0,1:T(8,128)(2,1)} %param.15), kind=kLoop, calls=%fused_computation.15 | loop fusion | bytes 5849092 | tf_op jit(solution)/shard_map/dynamic_slice | solution.py:850
  8.1 1.4 copy.45.refs_11_
  9.5 1.4 copy.44.refs_5_
  10.9 2.0 %shard_map.255 = bf16[256,1024]{1,0:T(8,128)(2,1)} custom-call(s32[3]{0:T(128)} %pad_add_fusion.place, bf16[1,256,1024]{2,1,0:T(8,128)(2,1)} %refs_1_.3, bf16[1,1024,256]{2,1,0:T(8,128)(2,1)} %dnw.1), custom_call_target="tpu_custom_call" | custom-call | tf_op jit(solution)/shard_map/pallas_call | solution.py:894
  13.0 0.3 collective-permute-done.refs_3_.refs_5_
  13.3 0.0 collective-permute-start.1
  13.3 1.7 collective-permute-start.2
  15.1 0.7 copy-done.6
  15.8 16.5 %shard_map.256 = (bf16[3072,256]{1,0:T(8,128)(2,1)}, bf16[3072,128]{1,0:T(8,128)(2,1)}, bf16[3072,256]{1,0:T(8,128)(2,1)}, bf16[256,3072]{1,0:T(8,128)(2,1)}, bf...) custom-call(s32[3]{0:T(128)} %pad_add_fusion.place, ...), custom_call_target="tpu_custom_call" | custom-call | flops 17999998976 | bytes 3000000 | tf_op jit(solution)/shard_map/pallas_call | solution.py:805
  32.3 0.3 collective-permute-start.3
  32.6 1.7 collective-permute-done.3.refs_8_
  34.3 0.8 copy-done.4
  35.1 51.2 %shard_map.257 = (bf16[3072,1024]{1,0:T(8,128)(2,1)}, bf16[3072,1024]{1,0:T(8,128)(2,1)}, bf16[3072,256]{1,0:T(8,128)(2,1)}, bf16[16,357,128]{2,1,0:T(8,128)(2,1...) custom-call(s32[3]{0:T(128)} %pad_add_fusion.place, ...), custom_call_target="tpu_custom_call" | custom-call | flops 71999995904 | bytes 3000000 | tf_op jit(solution)/shard_map/pallas_call | solution.py:805
  86.2 0.0 copy-start.1
  86.2 0.3 collective-permute-start.4
  86.5 2.1 %copy.38 = bf16[8,357,128]{2,0,1:T(8,128)(2,1)} copy(bf16[8,357,128]{2,1,0:T(8,128)(2,1)} %get-tuple-element.86) | data formatting | bytes 1462272 | tf_op jit(solution)/shard_map/pallas_call | solution.py:805
  88.6 1.5 collective-permute-start.5
  90.1 1.1 add_convert_fusion.1
  91.2 4.0 %all-to-all-start = ((bf16[8,416,128]{2,1,0:T(8,128)(2,1)}), bf16[8,416,128]{2,1,0:T(8,128)(2,1)S(1)}, u32[]{:S(2)}, u32[]{:S(2)}) async-start(bf16[8,416,128]{2,1,0:T(8,128)(2,1)} %bitcast.7), calls=%async_computation | async-start | bytes 1703936 | tf_op jit(solution)/shard_map/all_to_all | solution.py:867
  95.3 28.8 %shard_map.258 = (f32[16,357,128]{2,1,0:T(8,128)}, bf16[6,357,128]{2,1,0:T(8,128)(2,1)}, bf16[2,357,128]{2,1,0:T(8,128)(2,1)}, bf16[3328,128]{1,0:T(8,128)(2,1)}, bf16[3328,128]{1,0:T(8,128)(2,1)}) custom-call(s32[3]{0:T(128)} %pad_add_fusion.place, f32[1,3072]{1,0:T(1,128)} %get-tuple-element.72.refs_0_, bf16[256,768]{1,0:T(8,128)(2,1)} %bitcast.23, ...), custom_call_target="tpu_custom_call" | custom-call | flops 40000000000 | bytes 3000000 | tf_op jit(solution)/shard_map/pallas_call | solution.py:805
  124.1 0.1 collective-permute-start.6
  124.2 1.1 copy.39
  125.3 2.0 %collective-permute-start.7 = (bf16[2,357,128]{2,0,1:T(2,128)(2,1)S(1)}, bf16[2,357,128]{2,0,1:T(2,128)(2,1)S(1)}, u32[]{:S(2)}, u32[]{:S(2)}) collective-permute-start(bf16[2,357,128]{2,0,1:T(2,128)(2,1)S(1)} %copy.39), channel_id=1, source_target_pairs={{0,16},{16,0},{1,17},{17,1},{2,18},{18,2},{3,19},{19,3},{4,20},{20... | collective-permute-start | bytes 548360 | tf_op jit(solution)/shard_map/ppermute | solution.py:853
  127.3 2.3 %add_convert_fusion = bf16[3328,128]{1,0:T(8,128)(2,1)} fusion(bf16[3328,128]{1,0:T(8,128)(2,1)S(1)} %collective-permute-done.6, bf16[3328,128]{1,0:T(8,128)(2,1)} %get-tuple-element.103), kind=kLoop, calls=%fused_computation.2 | loop fusion | flops 1703936 | bytes 2555904 | tf_op jit(solution)/shard_map/convert_element_type | solution.py:973
  129.6 3.0 %collective-permute-done.7 = bf16[2,357,128]{2,0,1:T(2,128)(2,1)S(1)} collective-permute-done((bf16[2,357,128]{2,0,1:T(2,128)(2,1)S(1)}, bf16[2,357,128]{2,0,1:T(2,128)(2,1)S(1)}, u32[]{:S(2)}, u32[]{:S(2)}) %collective-permute-start.7) | collective-permute-done | bytes 182816 | tf_op jit(solution)/shard_map/ppermute | solution.py:853
  132.6 4.8 %all-to-all-start.1 = ((bf16[8,416,128]{2,1,0:T(8,128)(2,1)}), bf16[8,416,128]{2,1,0:T(8,128)(2,1)S(1)}, u32[]{:S(2)}, u32[]{:S(2)}) async-start(bf16[8,416,128]{2,1,0:T(8,128)(2,1)} %bitcast.8), calls=%async_computation.1 | async-start | bytes 1703936 | tf_op jit(solution)/shard_map/all_to_all | solution.py:867
  137.4 0.1 reduce_sum.25
  137.5 2.7 %collective-permute-start.10 = (bf16[416,128]{1,0:T(8,128)(2,1)S(1)}, bf16[416,128]{1,0:T(8,128)(2,1)S(1)}, u32[]{:S(2)}, u32[]{:S(2)}) collective-permute-start(bf16[416,128]{1,0:T(8,128)(2,1)S(1)} %reduce_sum.25), channel_id=1, source_target_pairs={{0,8},{1,9},{2,10},{3,11},{4,12},{5,13},{6,14},{7,15},{8,0},{9,1},... | collective-permute-start | bytes 319496 | tf_op jit(solution)/shard_map/ppermute | solution.py:870
  140.2 2.0 %collective-permute-start.9 = (bf16[6,357,128]{2,1,0:T(8,128)(2,1)}, bf16[6,357,128]{2,1,0:T(8,128)(2,1)S(1)}, u32[]{:S(2)}, u32[]{:S(2)}) collective-permute-start(bf16[6,357,128]{2,1,0:T(8,128)(2,1)} %get-tuple-element.109), channel_id=1, source_target_pairs={{0,16},{16,0},{1,17},{17,1},{2,18},{18,2},{3,19},{19,3},{4,20},{20... | collective-permute-start | bytes 1645064 | tf_op jit(solution)/shard_map/ppermute | solution.py:853
  142.2 3.1 %fusion.1 = bf16[357,16,128]{2,1,0:T(8,128)(2,1)} fusion(bf16[8,357,128]{2,0,1:T(8,128)(2,1)S(1)} %collective-permute-done.5, bf16[16,357,128]{2,1,0:T(8,128)(2,1)} %get-tuple-element.107, pred[16]{0:T(512)(128)(4,1)S(1)} %fusion.2), kind=kLoop, calls=%fused_computation.5 | loop fusion | flops 3655680 | bytes 3655696 | tf_op jit(solution)/shard_map/jit(_where)/select_n | solution.py:1052
  145.3 7.6 %all-to-all-done.1 = bf16[8,416,128]{2,1,0:T(8,128)(2,1)S(1)} async-done(((bf16[8,416,128]{2,1,0:T(8,128)(2,1)}), bf16[8,416,128]{2,1,0:T(8,128)(2,1)S(1)}, u32[]{:S(2)}, u32[]{:S(2)}) %all-to-all-start.1) | async-done | bytes 852000 | tf_op jit(solution)/shard_map/all_to_all | solution.py:867
  152.9 0.1 reduce_sum.24
  153.0 1.6 collective-permute-start.8
  154.6 4.6 %collective-permute-done.8 = bf16[416,128]{1,0:T(8,128)(2,1)S(1)} collective-permute-done((bf16[416,128]{1,0:T(8,128)(2,1)S(1)}, bf16[416,128]{1,0:T(8,128)(2,1)S(1)}, u32[]{:S(2)}, u32[]{:S(2)}) %collective-permute-start.8) | collective-permute-done | bytes 106528 | tf_op jit(solution)/shard_map/ppermute | solution.py:870
  159.3 1.5 collective-permute-done.9
  160.8 0.1 broadcast_in_dim.23
  160.8 0.1 broadcast_in_dim.22
  160.9 1.0 pad_maximum_fusion
  161.9 3.7 %all-to-all-start.2 = ((bf16[8,416,128]{2,1,0:T(8,128)(2,1)}), bf16[8,416,128]{2,1,0:T(8,128)(2,1)S(1)}, u32[]{:S(2)}, u32[]{:S(2)}) async-start(bf16[8,416,128]{2,1,0:T(8,128)(2,1)} %pad_maximum_fusion), calls=%async_computation.2 | async-start | bytes 1703936 | tf_op jit(solution)/shard_map/all_to_all | solution.py:867
  165.6 0.1 copy.41
  165.7 4.7 %fusion = f32[357,16,128]{2,1,0:T(8,128)} fusion(f32[16,357,128]{2,1,0:T(8,128)} %get-tuple-element.113, bf16[2,357,128]{2,0,1:T(2,128)(2,1)S(1)} %collective-permute-done.7, bf16[6,357,128]{2,0,1:T(8,128)(2,1)S(1)} %copy.41, pred[16]{0:T(512)(128)(4,1)S(1)} %fusion.2), kind=kLoop, calls=%fused_computation.1 | loop fusion | flops 6580224 | bytes 6580240 | tf_op jit(solution)/shard_map/jit(_where)/select_n | solution.py:1052
  170.4 8.6 %all-to-all-done.2 = bf16[8,416,128]{2,1,0:T(8,128)(2,1)S(1)} async-done(((bf16[8,416,128]{2,1,0:T(8,128)(2,1)}), bf16[8,416,128]{2,1,0:T(8,128)(2,1)S(1)}, u32[]{:S(2)}, u32[]{:S(2)}) %all-to-all-start.2) | async-done | bytes 852000 | tf_op jit(solution)/shard_map/all_to_all | solution.py:867
  179.0 2.4 %collective-permute-done.11 = bf16[8,416,128]{2,1,0:T(8,128)(2,1)S(1)} collective-permute-done((bf16[8,416,128]{2,1,0:T(8,128)(2,1)S(1)}, bf16[8,416,128]{2,1,0:T(8,128)(2,1)S(1)}, u32[]{:S(2)}, u32[]{:S(2)}) %collective-permute-start.11) | collective-permute-done | bytes 852000 | tf_op jit(solution)/shard_map/ppermute | solution.py:856
  181.4 1.0 copy-done.2
  182.3 4.7 %shard_map.259 = (f32[1,256]{1,0:T(1,128)}, f32[1,256]{1,0:T(1,128)}, f32[1,256,768]{2,1,0:T(8,128)}, f32[1,512]{1,0:T(1,128)}, f32[1,256,256]{2,1,0:T(8,128)}, ...) custom-call(s32[3]{0:T(128)} %pad_add_fusion.place, ...), custom_call_target="tpu_custom_call" | custom-call | tf_op jit(solution)/shard_map/pallas_call | solution.py:1083
  (21 shorter events, 0.1 us)
Async XLA Ops:
  3.2 10.2 %collective-permute-start = (bf16[144,1024]{1,0:T(8,128)(2,1)}, bf16[144,1024]{1,0:T(8,128)(2,1)S(1)}, u32[]{:S(2)}, u32[]{:S(2)}) collective-permute-start(bf16[144,1024]{1,0:T(8,128)(2,1)} %get-tuple-element.73), channel_id=1, source_target_pairs={{0,16},{16,0},{1,17},{17,1},{2,18},{18,2},{3,19},{19,3},{4,20},{20... | collective-permute-start | bytes 884744 | tf_op jit(solution)/shard_map/ppermute | solution.py:853
  13.3 1.8 copy-start.5
  13.3 1.8 collective-permute-start.1
  13.3 18.9 %collective-permute-start.2 = (bf16[256,1024]{1,0:T(8,128)(2,1)}, bf16[256,1024]{1,0:T(8,128)(2,1)S(1)}, u32[]{:S(2)}, u32[]{:S(2)}) collective-permute-start(bf16[256,1024]{1,0:T(8,128)(2,1)} %shard_map.255), channel_id=1, source_target_pairs={{0,16},{16,0},{1,17},{17,1},{2,18},{18,2},{3,19},{19,3},{4,20},{20... | collective-permute-start | bytes 1572872 | tf_op jit(solution)/shard_map/ppermute | solution.py:853
  15.1 0.7 copy-start.6
  32.3 2.0 %copy-start.3 = (bf16[256,1024]{1,0:T(8,128)(2,1)}, bf16[256,1024]{1,0:T(8,128)(2,1)S(1)}, u32[]{:S(2)}) copy-start(bf16[256,1024]{1,0:T(8,128)(2,1)S(1)} %collective-permute-done.2.refs_7_) | copy-start | bytes 1572868
  32.3 2.0 %collective-permute-start.3 = (bf16[256,1024]{1,0:T(8,128)(2,1)S(1)}, bf16[256,1024]{1,0:T(8,128)(2,1)S(1)}, u32[]{:S(2)}, u32[]{:S(2)}) collective-permute-start(bf16[256,1024]{1,0:T(8,128)(2,1)S(1)} %collective-permute-done.2.refs_7_), channel_id=1, source_target_pairs={{0,1},{1,0},{2,3},{3,2},{4,5},{5,4},{6,7},{7,6},{8,9},{9,8},{10,11... | collective-permute-start | bytes 1572872 | tf_op jit(solution)/shard_map/ppermute | solution.py:856
  34.3 0.8 copy-start.4
  86.2 3.9 %copy-start.1 = (bf16[3328,128]{1,0:T(8,128)(2,1)S(1)}, bf16[3328,128]{1,0:T(8,128)(2,1)}, u32[]{:S(2)}) copy-start(bf16[3328,128]{1,0:T(8,128)(2,1)} %get-tuple-element.82) | copy-start | bytes 2555908
  86.2 3.9 %collective-permute-start.4 = (bf16[3328,128]{1,0:T(8,128)(2,1)}, bf16[3328,128]{1,0:T(8,128)(2,1)S(1)}, u32[]{:S(2)}, u32[]{:S(2)}) collective-permute-start(bf16[3328,128]{1,0:T(8,128)(2,1)} %get-tuple-element.83), channel_id=1, source_target_pairs={{0,1},{1,0},{2,3},{3,2},{4,5},{5,4},{6,7},{7,6},{8,9},{9,8},{10,11... | collective-permute-start | bytes 2555912 | tf_op jit(solution)/shard_map/ppermute | solution.py:856
  88.6 35.5 %collective-permute-start.5 = (bf16[8,357,128]{2,0,1:T(8,128)(2,1)}, bf16[8,357,128]{2,0,1:T(8,128)(2,1)S(1)}, u32[]{:S(2)}, u32[]{:S(2)}) collective-permute-start(bf16[8,357,128]{2,0,1:T(8,128)(2,1)} %copy.38), channel_id=1, source_target_pairs={{0,16},{16,0},{1,17},{17,1},{2,18},{18,2},{3,19},{19,3},{4,20},{20... | collective-permute-start | bytes 2193416 | tf_op jit(solution)/shard_map/ppermute | solution.py:853
  91.2 32.9 %all-to-all-start = ((bf16[8,416,128]{2,1,0:T(8,128)(2,1)}), bf16[8,416,128]{2,1,0:T(8,128)(2,1)S(1)}, u32[]{:S(2)}, u32[]{:S(2)}) async-start(bf16[8,416,128]{2,1,0:T(8,128)(2,1)} %bitcast.7), calls=%async_computation | async-start | bytes 1703936 | tf_op jit(solution)/shard_map/all_to_all | solution.py:867
  124.1 3.2 %collective-permute-start.6 = (bf16[3328,128]{1,0:T(8,128)(2,1)}, bf16[3328,128]{1,0:T(8,128)(2,1)S(1)}, u32[]{:S(2)}, u32[]{:S(2)}) collective-permute-start(bf16[3328,128]{1,0:T(8,128)(2,1)} %get-tuple-element.104), channel_id=1, source_target_pairs={{0,1},{1,0},{2,3},{3,2},{4,5},{5,4},{6,7},{7,6},{8,9},{9,8},{10,11... | collective-permute-start | bytes 2555912 | tf_op jit(solution)/shard_map/ppermute | solution.py:856
  125.3 7.3 %collective-permute-start.7 = (bf16[2,357,128]{2,0,1:T(2,128)(2,1)S(1)}, bf16[2,357,128]{2,0,1:T(2,128)(2,1)S(1)}, u32[]{:S(2)}, u32[]{:S(2)}) collective-permute-start(bf16[2,357,128]{2,0,1:T(2,128)(2,1)S(1)} %copy.39), channel_id=1, source_target_pairs={{0,16},{16,0},{1,17},{17,1},{2,18},{18,2},{3,19},{19,3},{4,20},{20... | collective-permute-start | bytes 548360 | tf_op jit(solution)/shard_map/ppermute | solution.py:853
  132.6 20.3 %all-to-all-start.1 = ((bf16[8,416,128]{2,1,0:T(8,128)(2,1)}), bf16[8,416,128]{2,1,0:T(8,128)(2,1)S(1)}, u32[]{:S(2)}, u32[]{:S(2)}) async-start(bf16[8,416,128]{2,1,0:T(8,128)(2,1)} %bitcast.8), calls=%async_computation.1 | async-start | bytes 1703936 | tf_op jit(solution)/shard_map/all_to_all | solution.py:867
  137.5 17.1 %collective-permute-start.10 = (bf16[416,128]{1,0:T(8,128)(2,1)S(1)}, bf16[416,128]{1,0:T(8,128)(2,1)S(1)}, u32[]{:S(2)}, u32[]{:S(2)}) collective-permute-start(bf16[416,128]{1,0:T(8,128)(2,1)S(1)} %reduce_sum.25), channel_id=1, source_target_pairs={{0,8},{1,9},{2,10},{3,11},{4,12},{5,13},{6,14},{7,15},{8,0},{9,1},... | collective-permute-start | bytes 319496 | tf_op jit(solution)/shard_map/ppermute | solution.py:870
  140.2 20.6 %collective-permute-start.9 = (bf16[6,357,128]{2,1,0:T(8,128)(2,1)}, bf16[6,357,128]{2,1,0:T(8,128)(2,1)S(1)}, u32[]{:S(2)}, u32[]{:S(2)}) collective-permute-start(bf16[6,357,128]{2,1,0:T(8,128)(2,1)} %get-tuple-element.109), channel_id=1, source_target_pairs={{0,16},{16,0},{1,17},{17,1},{2,18},{18,2},{3,19},{19,3},{4,20},{20... | collective-permute-start | bytes 1645064 | tf_op jit(solution)/shard_map/ppermute | solution.py:853
  153.0 6.2 %collective-permute-start.8 = (bf16[416,128]{1,0:T(8,128)(2,1)S(1)}, bf16[416,128]{1,0:T(8,128)(2,1)S(1)}, u32[]{:S(2)}, u32[]{:S(2)}) collective-permute-start(bf16[416,128]{1,0:T(8,128)(2,1)S(1)} %reduce_sum.24), channel_id=1, source_target_pairs={{0,8},{1,9},{2,10},{3,11},{4,12},{5,13},{6,14},{7,15},{8,0},{9,1},... | collective-permute-start | bytes 319496 | tf_op jit(solution)/shard_map/ppermute | solution.py:870
  161.9 17.1 %all-to-all-start.2 = ((bf16[8,416,128]{2,1,0:T(8,128)(2,1)}), bf16[8,416,128]{2,1,0:T(8,128)(2,1)S(1)}, u32[]{:S(2)}, u32[]{:S(2)}) async-start(bf16[8,416,128]{2,1,0:T(8,128)(2,1)} %pad_maximum_fusion), calls=%async_computation.2 | async-start | bytes 1703936 | tf_op jit(solution)/shard_map/all_to_all | solution.py:867
  179.0 2.4 %copy-start = (bf16[8,416,128]{2,1,0:T(8,128)(2,1)}, bf16[8,416,128]{2,1,0:T(8,128)(2,1)S(1)}, u32[]{:S(2)}) copy-start(bf16[8,416,128]{2,1,0:T(8,128)(2,1)S(1)} %all-to-all-done.2) | copy-start | bytes 2555908
  179.0 2.4 %collective-permute-start.11 = (bf16[8,416,128]{2,1,0:T(8,128)(2,1)S(1)}, bf16[8,416,128]{2,1,0:T(8,128)(2,1)S(1)}, u32[]{:S(2)}, u32[]{:S(2)}) collective-permute-start(bf16[8,416,128]{2,1,0:T(8,128)(2,1)S(1)} %all-to-all-done.2), channel_id=1, source_target_pairs={{0,1},{1,0},{2,3},{3,2},{4,5},{5,4},{6,7},{7,6},{8,9},{9,8},{10,11... | collective-permute-start | bytes 2555912 | tf_op jit(solution)/shard_map/ppermute | solution.py:856
  181.4 1.0 copy-start.2

commit v2 on v1

--- a/solution.py
+++ b/solution.py
@@ -163,19 +163,20 @@
 
     def scores(u):
         p, member = units[u]
-        for t, (at, stop, _) in enumerate(TILES):
-            T.s[u % 3, 0:stop, 256 * t : 256 * t + 256] = dot_upper(
+        for t, (at, stop, sure) in enumerate(TILES):
+            lanes = slice(256 * t, 256 * t + 256)
+            both = dot_upper(
                 T.k[of(member, 0, stop), 128 * p : 128 * p + 128],
                 two_heads(S.q, p, of(member, at, at + 128)),
             )
+            if sure:
+                T.s[u % 3, 0:sure, lanes] = both[0:sure]
+            mask = twice(T.mask[member, t, 0 : stop - sure, :])
+            T.s[u % 3, sure:stop, lanes] = both[sure:stop] + mask
 
     def strips(u, t, side):
-        _, stop, sure = TILES[t]
-        for start in range(0, stop, 16):
-            value = T.s[u % 3, start : start + 16, column_of(t, side)]
-            if start >= sure:
-                value = value + T.mask[units[u][1], t, start - sure : start - sure + 16, :]
-            yield start, value
+        for start in range(0, TILES[t][1], 16):
+            yield start, T.s[u % 3, start : start + 16, column_of(t, side)]
 
     columns = [(t, side) for t in range(3) for side in range(2)]
 
@@ -518,14 +519,14 @@
             emit_half(refs.send, 0, 1 - half, refs)
 
 
-def pack_kernel(place, *refs):
+def pack_kernel(*refs):
     vec, half = refs[-2:]
     inw, outw = refs[8:10]
     at = 0
     for ref in refs[:8]:
         vec[:, at : at + ref.shape[1]] = ref[...]
         at += ref.shape[1]
-    rows = pl.ds(pl.multiple_of(place[2] * 128, 128), 128)
+    rows = pl.ds(pl.multiple_of(lax.axis_index("batch") % 2 * 128, 128), 128)
     half[0:128, 0:768] = inw[0, rows, :]
     half[0:128, 768:1024] = outw[0, rows, :]
     rest = jnp.concatenate([vec[:, 1024 * j : 1024 * j + 1024] for j in range(3)], axis=0)
@@ -538,10 +539,11 @@
     half[128:144, :] = jnp.concatenate(parts, axis=0).astype(bf16)
 
 
-def pack_feed_kernel(place, upw, dnw, half):
-    half[0:128, :] = upw[0, pl.ds(pl.multiple_of(place[2] * 128, 128), 128), :]
+def pack_feed_kernel(upw, dnw, half):
+    core = lax.axis_index("batch") % 2
+    half[0:128, :] = upw[0, pl.ds(pl.multiple_of(core * 128, 128), 128), :]
     for j in range(4):
-        rows = pl.ds(pl.multiple_of(place[2] * 512 + 128 * j, 128), 128)
+        rows = pl.ds(pl.multiple_of(core * 512 + 128 * j, 128), 128)
         half[128:256, 256 * j : 256 * j + 256] = dnw[0, rows, :]
 
 
@@ -702,14 +704,25 @@
     return jnp.broadcast_to(value, (256, 128)).T[0:1]
 
 
-def finish(halves, inw, upw, again, ashift, mgain, mshift, outs):
-    ga, sa, giw, gib, gow, gob, gm, sm, guw, gub, gdw, gdb = outs
+def finish(halves, weights, vectors, small, large, copies):
+    again, ashift, mgain, mshift = vectors
+    ga, sa, gib, gob, gm, sm, gub, gdb = small
+    giw, gow, guw, gdw = large
+    inw, upw = weights
+    fetch_inw, fetch_upw, send_giw, send_gow, send_guw, send_gdw = copies
 
     def block(half, at, count, part):
         start, tail = at + 256 * part, at + 512 * count + ONES * part
         rows = halves[half][start : start + 256, :].astype(f32)
         return rows, halves[half][tail : tail + ONES, :].astype(f32)[0:1]
 
+    for part in range(8):
+        rows, sums = block(1, 0, 4, part)
+        gdw[0, 128 * part : 128 * part + 128, :] = rows.T
+        if part < 2:
+            gdb[:, 128 * part : 128 * part + 128] = sums
+    send_gdw.start()
+    fetch_upw.wait()
     gain, shift = column(mgain[...]), column(mshift[...])
     of_gain, of_shift = [], []
     for part in range(8):
@@ -720,13 +733,10 @@
         weight = upw[0, :, lanes].astype(f32)
         of_gain.append(weight * rows)
         of_shift.append(weight * sums)
+    send_guw.start()
     gm[...] = line(jnp.sum(tree(jnp.add, of_gain), axis=1, keepdims=True))
     sm[...] = line(jnp.sum(tree(jnp.add, of_shift), axis=1, keepdims=True))
-    for part in range(8):
-        rows, sums = block(1, 0, 4, part)
-        gdw[0, 128 * part : 128 * part + 128, :] = rows.T
-        if part < 2:
-            gdb[:, 128 * part : 128 * part + 128] = sums
+    fetch_inw.wait()
     gain, shift = column(again[...]), column(ashift[...])
     of_gain, of_shift = [], []
     for part in range(8):
@@ -745,20 +755,32 @@
             lanes = slice(128 * (part - 6), 128 * (part - 6) + 128)
             gow[0, :, lanes] = rows
             gob[:, lanes] = sums
+    send_giw.start()
+    send_gow.start()
     ga[...] = line(jnp.sum(tree(jnp.add, of_gain), axis=1, keepdims=True))
     sa[...] = line(jnp.sum(tree(jnp.add, of_shift), axis=1, keepdims=True))
-
-
-def final_kernel(place, own, far, *refs):
-    weights, outs = refs[:6], refs[6:]
+    for copy in (send_giw, send_gow, send_guw, send_gdw):
+        copy.wait()
+
+
+def final_kernel(place, own, far, inw, upw, again, ashift, mgain, mshift, *refs):
+    ga, sa, giw, gib, gow, gob, gm, sm, guw, gub, gdw, gdb = refs[:12]
+    *held, sem = refs[12:]
+    pairs = [(inw, held[0]), (upw, held[1])]
+    pairs += list(zip(held[2:], (giw, gow, guw, gdw)))
+    copies = [pltpu.make_async_copy(a, b, sem.at[i]) for i, (a, b) in enumerate(pairs)]
+    copies[0].start()
+    copies[1].start()
+    vectors = (again, ashift, mgain, mshift)
+    small = (ga, sa, gib, gob, gm, sm, gub, gdb)
 
     @pl.when(place[2] == 0)
     def _():
-        finish((own, far), *weights, outs)
+        finish((own, far), held[:2], vectors, small, held[2:], copies)
 
     @pl.when(place[2] != 0)
     def _():
-        finish((far, own), *weights, outs)
+        finish((far, own), held[:2], vectors, small, held[2:], copies)
 
 
 SMEM = pl.BlockSpec(memory_space=pltpu.SMEM)
@@ -871,14 +893,13 @@
 
     vectors, half_weights = pl.pallas_call(
         pack_kernel,
-        in_specs=[SMEM] + [VMEM] * 10,
+        in_specs=[VMEM] * 10,
         out_specs=[VMEM] * 2,
         out_shape=[
             jax.ShapeDtypeStruct((1, 3072), f32),
             jax.ShapeDtypeStruct((144, 1024), bf16),
         ],
     )(
-        place,
         attend_gain,
         attend_shift,
         inward_bias,
@@ -893,10 +914,10 @@
     own_attend = (vectors, inward_weight[0], outward_weight[0])
     half_feed = pl.pallas_call(
         pack_feed_kernel,
-        in_specs=[SMEM] + [VMEM] * 2,
+        in_specs=[VMEM] * 2,
         out_specs=VMEM,
         out_shape=jax.ShapeDtypeStruct((256, 1024), bf16),
-    )(place, up_weight, down_weight)
+    )(up_weight, down_weight)
     arrived, half_feed, held_tokens, held_cotangent = lax.optimization_barrier(
         (across(half_weights), half_feed, mine(tokens), mine(cotangent))
     )
@@ -1082,9 +1103,18 @@
     )
     finals = pl.pallas_call(
         final_kernel,
-        in_specs=[SMEM] + [VMEM] * 8,
-        out_specs=[VMEM] * 12,
+        in_specs=[SMEM] + [VMEM] * 2 + [ANY] * 2 + [VMEM] * 4,
+        out_specs=[ANY if len(shape) == 3 else VMEM for shape in grads],
         out_shape=[jax.ShapeDtypeStruct(shape, f32) for shape in grads],
+        scratch_shapes=[
+            pltpu.VMEM((1, 256, 768), bf16),
+            pltpu.VMEM((1, 256, 1024), bf16),
+            pltpu.VMEM((1, 256, 768), f32),
+            pltpu.VMEM((1, 256, 256), f32),
+            pltpu.VMEM((1, 256, 1024), f32),
+            pltpu.VMEM((1, 1024, 256), f32),
+            pltpu.SemaphoreType.DMA((6,)),
+        ],
         compiler_params=pltpu.CompilerParams(vmem_limit_bytes=VMEM_LIMIT),
     )(
         place,

time: 188 us -> 189 us (level)
  transfers between devices with their start and end apart: 15 -> 15, of which waited for: 8 -> 8; matrix products, arithmetic and copies ran while one was open for 10% -> 11% of each run, Pallas kernels for 25% -> 25%
where the time goes in v2:
time: 189 us; the launch traced here: 188 us
  Pallas kernels  106 us (56%)
  waiting for transfers between devices  29.7 us (16%)
  starting transfers between devices  27.6 us (15%)
  other arithmetic  13 us (7%)
  local copies, waits for them, and re-layouts  10.7 us (6%)
    pallas_call x3, Pallas kernels, call(): pl.pallas_call(run, grid_spec=pltpu.PrefetchScalarGridSpec(num_scalar_pre...  96.5 us
    all_to_all x3, waiting for transfers between devices, exchange(): lax.all_to_all(value, everyone, 0, 0, tiled=True, axis_index_groups=cubes)  16.2 us
    all_to_all x3, starting transfers between devices, exchange(): lax.all_to_all(value, everyone, 0, 0, tiled=True, axis_index_groups=cubes)  13.1 us
    ppermute x5, starting transfers between devices, across(): return lax.ppermute(value, 'section', ((0, 1), (1, 0)))  9.63 us
    select_n x2, other arithmetic, assemble(): value = jnp.where(ours, held.transpose(1, 0, 2), arrived.transpose(1, 0, 2))  7.76 us
    pallas_call x1, Pallas kernels, body(): pl.pallas_call(final_kernel, in_specs=[SMEM] + [VMEM] * 2 + [ANY] * 2 + [...  5.33 us
    ppermute x5, waiting for transfers between devices, across(): return lax.ppermute(value, 'section', ((0, 1), (1, 0)))  4.85 us
    ppermute x2, waiting for transfers between devices, partner(): return lax.ppermute(value, 'batch', [(b, b ^ flip) for b in range(batches)])  4.6 us
  transfers between devices with their start and end apart: 15, of which 8 were waited for; matrix products, arithmetic and copies ran while one was open for 11% of the time, Pallas kernels for 25%

profile of v2, /device:TPU:0, one launch (start us, length us, event | category | flops | bytes accessed | tf_op | source)
XLA Modules:
  0.0 187.8 jit_solution(4363524346940192968)
XLA Ops:
  0.6 1.9 %shard_map.254 = (f32[1,3072]{1,0:T(1,128)}, bf16[144,1024]{1,0:T(8,128)(2,1)}) custom-call(f32[1,256]{1,0:T(1,128)} %again.1, f32[1,256]{1,0:T(1,128)} %ashift.1, f32[1,512]{1,0:T(1,128)} %refs_2_.1, f32[1,256]{1,0:T(1,128)} %refs_3_.1, f32[1,256]{1,0:T(1,128)} %mgain.1, f32[1,256]{1,0:T(1,128)} %mshift.1, f32[1,1024]{1,0:T(1,128)} %refs_6_.2, ...), custom_call_target="tpu_custom_call" | custom-call | tf_op jit(solution)/shard_map/pallas_call | solution.py:894
  2.6 2.9 %collective-permute-start = (bf16[144,1024]{1,0:T(8,128)(2,1)}, bf16[144,1024]{1,0:T(8,128)(2,1)S(1)}, u32[]{:S(2)}, u32[]{:S(2)}) collective-permute-start(bf16[144,1024]{1,0:T(8,128)(2,1)} %get-tuple-element.73), channel_id=1, source_target_pairs={{0,16},{16,0},{1,17},{17,1},{2,18},{18,2},{3,19},{19,3},{4,20},{20... | collective-permute-start | bytes 884744 | tf_op jit(solution)/shard_map/ppermute | solution.py:875
  5.5 2.0 %constant_dynamic-slice_fusion = (bf16[8,357,256]{2,0,1:T(8,128)(2,1)S(1)}, bf16[8,357,256]{2,0,1:T(8,128)(2,1)S(1)}) fusion(bf16[16,357,256]{2,0,1:T(8,128)(2,1)} %param.16, s32[]{:T(128)S(6)} %select_n.35, bf16[16,357,256]{2,0,1:T(8,128)(2,1)} %param.15), kind=kLoop, calls=%fused_computation.15 | loop fusion | bytes 5849092 | tf_op jit(solution)/shard_map/dynamic_slice | solution.py:872
  7.5 1.4 copy.45.refs_11_
  8.9 1.4 copy.44.refs_5_
  10.3 2.0 %shard_map.255 = bf16[256,1024]{1,0:T(8,128)(2,1)} custom-call(bf16[1,256,1024]{2,1,0:T(8,128)(2,1)} %upw.3, bf16[1,1024,256]{2,1,0:T(8,128)(2,1)} %dnw.1), custom_call_target="tpu_custom_call" | custom-call | tf_op jit(solution)/shard_map/pallas_call | solution.py:915
  12.3 0.4 collective-permute-done.refs_3_.refs_5_
  12.7 0.0 collective-permute-start.1
  12.7 0.6 pad_add_fusion.place
  13.3 1.7 collective-permute-start.2
  15.1 0.7 copy-done.6
  15.8 16.5 %shard_map.256 = (bf16[3072,256]{1,0:T(8,128)(2,1)}, bf16[3072,128]{1,0:T(8,128)(2,1)}, bf16[3072,256]{1,0:T(8,128)(2,1)}, bf16[256,3072]{1,0:T(8,128)(2,1)}, bf...) custom-call(s32[3]{0:T(128)} %pad_add_fusion.place, ...), custom_call_target="tpu_custom_call" | custom-call | flops 17999998976 | bytes 3000000 | tf_op jit(solution)/shard_map/pallas_call | solution.py:827
  32.3 0.3 collective-permute-start.3
  32.6 1.7 collective-permute-done.3.refs_8_
  34.3 0.8 copy-done.4
  35.0 51.2 %shard_map.257 = (bf16[3072,1024]{1,0:T(8,128)(2,1)}, bf16[3072,1024]{1,0:T(8,128)(2,1)}, bf16[3072,256]{1,0:T(8,128)(2,1)}, bf16[16,357,128]{2,1,0:T(8,128)(2,1...) custom-call(s32[3]{0:T(128)} %pad_add_fusion.place, ...), custom_call_target="tpu_custom_call" | custom-call | flops 71999995904 | bytes 3000000 | tf_op jit(solution)/shard_map/pallas_call | solution.py:827
  86.2 0.0 copy-start.1
  86.3 0.3 collective-permute-start.4
  86.5 2.1 %copy.38 = bf16[8,357,128]{2,0,1:T(8,128)(2,1)} copy(bf16[8,357,128]{2,1,0:T(8,128)(2,1)} %get-tuple-element.86) | data formatting | bytes 1462272 | tf_op jit(solution)/shard_map/pallas_call | solution.py:827
  88.6 0.9 collective-permute-start.5
  89.5 1.1 add_convert_fusion.1
  90.6 4.6 %all-to-all-start = ((bf16[8,416,128]{2,1,0:T(8,128)(2,1)}), bf16[8,416,128]{2,1,0:T(8,128)(2,1)S(1)}, u32[]{:S(2)}, u32[]{:S(2)}) async-start(bf16[8,416,128]{2,1,0:T(8,128)(2,1)} %bitcast.7), calls=%async_computation | async-start | bytes 1703936 | tf_op jit(solution)/shard_map/all_to_all | solution.py:889
  95.2 28.8 %shard_map.258 = (f32[16,357,128]{2,1,0:T(8,128)}, bf16[6,357,128]{2,1,0:T(8,128)(2,1)}, bf16[2,357,128]{2,1,0:T(8,128)(2,1)}, bf16[3328,128]{1,0:T(8,128)(2,1)}, bf16[3328,128]{1,0:T(8,128)(2,1)}) custom-call(s32[3]{0:T(128)} %pad_add_fusion.place, f32[1,3072]{1,0:T(1,128)} %get-tuple-element.72.refs_0_, bf16[256,768]{1,0:T(8,128)(2,1)} %bitcast.23, ...), custom_call_target="tpu_custom_call" | custom-call | flops 40000000000 | bytes 3000000 | tf_op jit(solution)/shard_map/pallas_call | solution.py:827
  124.1 0.1 collective-permute-start.6
  124.2 1.1 copy.39
  125.3 2.0 %collective-permute-start.7 = (bf16[2,357,128]{2,0,1:T(2,128)(2,1)S(1)}, bf16[2,357,128]{2,0,1:T(2,128)(2,1)S(1)}, u32[]{:S(2)}, u32[]{:S(2)}) collective-permute-start(bf16[2,357,128]{2,0,1:T(2,128)(2,1)S(1)} %copy.39), channel_id=1, source_target_pairs={{0,16},{16,0},{1,17},{17,1},{2,18},{18,2},{3,19},{19,3},{4,20},{20... | collective-permute-start | bytes 548360 | tf_op jit(solution)/shard_map/ppermute | solution.py:875
  127.3 2.3 %add_convert_fusion = bf16[3328,128]{1,0:T(8,128)(2,1)} fusion(bf16[3328,128]{1,0:T(8,128)(2,1)S(1)} %collective-permute-done.6, bf16[3328,128]{1,0:T(8,128)(2,1)} %get-tuple-element.103), kind=kLoop, calls=%fused_computation.2 | loop fusion | flops 1703936 | bytes 2555904 | tf_op jit(solution)/shard_map/convert_element_type | solution.py:994
  129.6 3.0 %collective-permute-done.7 = bf16[2,357,128]{2,0,1:T(2,128)(2,1)S(1)} collective-permute-done((bf16[2,357,128]{2,0,1:T(2,128)(2,1)S(1)}, bf16[2,357,128]{2,0,1:T(2,128)(2,1)S(1)}, u32[]{:S(2)}, u32[]{:S(2)}) %collective-permute-start.7) | collective-permute-done | bytes 182816 | tf_op jit(solution)/shard_map/ppermute | solution.py:875
  132.5 4.8 %all-to-all-start.1 = ((bf16[8,416,128]{2,1,0:T(8,128)(2,1)}), bf16[8,416,128]{2,1,0:T(8,128)(2,1)S(1)}, u32[]{:S(2)}, u32[]{:S(2)}) async-start(bf16[8,416,128]{2,1,0:T(8,128)(2,1)} %bitcast.8), calls=%async_computation.1 | async-start | bytes 1703936 | tf_op jit(solution)/shard_map/all_to_all | solution.py:889
  137.4 0.1 reduce_sum.25
  137.5 2.7 %collective-permute-start.10 = (bf16[416,128]{1,0:T(8,128)(2,1)S(1)}, bf16[416,128]{1,0:T(8,128)(2,1)S(1)}, u32[]{:S(2)}, u32[]{:S(2)}) collective-permute-start(bf16[416,128]{1,0:T(8,128)(2,1)S(1)} %reduce_sum.25), channel_id=1, source_target_pairs={{0,8},{1,9},{2,10},{3,11},{4,12},{5,13},{6,14},{7,15},{8,0},{9,1},... | collective-permute-start | bytes 319496 | tf_op jit(solution)/shard_map/ppermute | solution.py:892
  140.2 2.0 %collective-permute-start.9 = (bf16[6,357,128]{2,1,0:T(8,128)(2,1)}, bf16[6,357,128]{2,1,0:T(8,128)(2,1)S(1)}, u32[]{:S(2)}, u32[]{:S(2)}) collective-permute-start(bf16[6,357,128]{2,1,0:T(8,128)(2,1)} %get-tuple-element.109), channel_id=1, source_target_pairs={{0,16},{16,0},{1,17},{17,1},{2,18},{18,2},{3,19},{19,3},{4,20},{20... | collective-permute-start | bytes 1645064 | tf_op jit(solution)/shard_map/ppermute | solution.py:875
  142.2 3.1 %fusion.1 = bf16[357,16,128]{2,1,0:T(8,128)(2,1)} fusion(bf16[8,357,128]{2,0,1:T(8,128)(2,1)S(1)} %collective-permute-done.5, bf16[16,357,128]{2,1,0:T(8,128)(2,1)} %get-tuple-element.107, pred[16]{0:T(512)(128)(4,1)S(1)} %fusion.2), kind=kLoop, calls=%fused_computation.5 | loop fusion | flops 3655680 | bytes 3655696 | tf_op jit(solution)/shard_map/jit(_where)/select_n | solution.py:1073
  145.3 7.6 %all-to-all-done.1 = bf16[8,416,128]{2,1,0:T(8,128)(2,1)S(1)} async-done(((bf16[8,416,128]{2,1,0:T(8,128)(2,1)}), bf16[8,416,128]{2,1,0:T(8,128)(2,1)S(1)}, u32[]{:S(2)}, u32[]{:S(2)}) %all-to-all-start.1) | async-done | bytes 852000 | tf_op jit(solution)/shard_map/all_to_all | solution.py:889
  152.9 0.1 reduce_sum.24
  153.0 1.6 collective-permute-start.8
  154.6 4.6 %collective-permute-done.8 = bf16[416,128]{1,0:T(8,128)(2,1)S(1)} collective-permute-done((bf16[416,128]{1,0:T(8,128)(2,1)S(1)}, bf16[416,128]{1,0:T(8,128)(2,1)S(1)}, u32[]{:S(2)}, u32[]{:S(2)}) %collective-permute-start.8) | collective-permute-done | bytes 106528 | tf_op jit(solution)/shard_map/ppermute | solution.py:892
  159.2 1.5 collective-permute-done.9
  160.7 0.1 broadcast_in_dim.23
  160.8 0.1 broadcast_in_dim.22
  160.9 1.0 pad_maximum_fusion
  161.8 3.7 %all-to-all-start.2 = ((bf16[8,416,128]{2,1,0:T(8,128)(2,1)}), bf16[8,416,128]{2,1,0:T(8,128)(2,1)S(1)}, u32[]{:S(2)}, u32[]{:S(2)}) async-start(bf16[8,416,128]{2,1,0:T(8,128)(2,1)} %pad_maximum_fusion), calls=%async_computation.2 | async-start | bytes 1703936 | tf_op jit(solution)/shard_map/all_to_all | solution.py:889
  165.5 0.1 copy.41
  165.7 4.7 %fusion = f32[357,16,128]{2,1,0:T(8,128)} fusion(f32[16,357,128]{2,1,0:T(8,128)} %get-tuple-element.113, bf16[2,357,128]{2,0,1:T(2,128)(2,1)S(1)} %collective-permute-done.7, bf16[6,357,128]{2,0,1:T(8,128)(2,1)S(1)} %copy.41, pred[16]{0:T(512)(128)(4,1)S(1)} %fusion.2), kind=kLoop, calls=%fused_computation.1 | loop fusion | flops 6580224 | bytes 6580240 | tf_op jit(solution)/shard_map/jit(_where)/select_n | solution.py:1073
  170.4 8.6 %all-to-all-done.2 = bf16[8,416,128]{2,1,0:T(8,128)(2,1)S(1)} async-done(((bf16[8,416,128]{2,1,0:T(8,128)(2,1)}), bf16[8,416,128]{2,1,0:T(8,128)(2,1)S(1)}, u32[]{:S(2)}, u32[]{:S(2)}) %all-to-all-start.2) | async-done | bytes 852000 | tf_op jit(solution)/shard_map/all_to_all | solution.py:889
  179.0 2.4 %collective-permute-done.11 = bf16[8,416,128]{2,1,0:T(8,128)(2,1)S(1)} collective-permute-done((bf16[8,416,128]{2,1,0:T(8,128)(2,1)S(1)}, bf16[8,416,128]{2,1,0:T(8,128)(2,1)S(1)}, u32[]{:S(2)}, u32[]{:S(2)}) %collective-permute-start.11) | collective-permute-done | bytes 852000 | tf_op jit(solution)/shard_map/ppermute | solution.py:878
  181.3 1.0 copy-done.2
  182.3 5.3 %shard_map.259 = (f32[1,256]{1,0:T(1,128)}, f32[1,256]{1,0:T(1,128)}, f32[1,256,768]{2,1,0:T(8,128)}, f32[1,512]{1,0:T(1,128)}, f32[1,256,256]{2,1,0:T(8,128)}, ...) custom-call(s32[3]{0:T(128)} %pad_add_fusion.place, ...), custom_call_target="tpu_custom_call" | custom-call | tf_op jit(solution)/shard_map/pallas_call | solution.py:1104
  (21 shorter events, 0.1 us)
Async XLA Ops:
  2.6 10.2 %collective-permute-start = (bf16[144,1024]{1,0:T(8,128)(2,1)}, bf16[144,1024]{1,0:T(8,128)(2,1)S(1)}, u32[]{:S(2)}, u32[]{:S(2)}) collective-permute-start(bf16[144,1024]{1,0:T(8,128)(2,1)} %get-tuple-element.73), channel_id=1, source_target_pairs={{0,16},{16,0},{1,17},{17,1},{2,18},{18,2},{3,19},{19,3},{4,20},{20... | collective-permute-start | bytes 884744 | tf_op jit(solution)/shard_map/ppermute | solution.py:875
  12.7 2.4 %copy-start.5 = (bf16[144,1024]{1,0:T(8,128)(2,1)}, bf16[144,1024]{1,0:T(8,128)(2,1)S(1)}, u32[]{:S(2)}) copy-start(bf16[144,1024]{1,0:T(8,128)(2,1)S(1)} %collective-permute-done.refs_3_.refs_5_) | copy-start | bytes 884740
  12.7 2.4 %collective-permute-start.1 = (bf16[144,1024]{1,0:T(8,128)(2,1)S(1)}, bf16[144,1024]{1,0:T(8,128)(2,1)S(1)}, u32[]{:S(2)}, u32[]{:S(2)}) collective-permute-start(bf16[144,1024]{1,0:T(8,128)(2,1)S(1)} %collective-permute-done.refs_3_.refs_5_), channel_id=1, source_target_pairs={{0,1},{1,0},{2,3},{3,2},{4,5},{5,4},{6,7},{7,6},{8,9},{9,8},{10,11... | collective-permute-start | bytes 884744 | tf_op jit(solution)/shard_map/ppermute | solution.py:878
  13.3 18.9 %collective-permute-start.2 = (bf16[256,1024]{1,0:T(8,128)(2,1)}, bf16[256,1024]{1,0:T(8,128)(2,1)S(1)}, u32[]{:S(2)}, u32[]{:S(2)}) collective-permute-start(bf16[256,1024]{1,0:T(8,128)(2,1)} %shard_map.255), channel_id=1, source_target_pairs={{0,16},{16,0},{1,17},{17,1},{2,18},{18,2},{3,19},{19,3},{4,20},{20... | collective-permute-start | bytes 1572872 | tf_op jit(solution)/shard_map/ppermute | solution.py:875
  15.1 0.7 copy-start.6
  32.3 2.0 %copy-start.3 = (bf16[256,1024]{1,0:T(8,128)(2,1)}, bf16[256,1024]{1,0:T(8,128)(2,1)S(1)}, u32[]{:S(2)}) copy-start(bf16[256,1024]{1,0:T(8,128)(2,1)S(1)} %collective-permute-done.2.refs_7_) | copy-start | bytes 1572868
  32.3 2.0 %collective-permute-start.3 = (bf16[256,1024]{1,0:T(8,128)(2,1)S(1)}, bf16[256,1024]{1,0:T(8,128)(2,1)S(1)}, u32[]{:S(2)}, u32[]{:S(2)}) collective-permute-start(bf16[256,1024]{1,0:T(8,128)(2,1)S(1)} %collective-permute-done.2.refs_7_), channel_id=1, source_target_pairs={{0,1},{1,0},{2,3},{3,2},{4,5},{5,4},{6,7},{7,6},{8,9},{9,8},{10,11... | collective-permute-start | bytes 1572872 | tf_op jit(solution)/shard_map/ppermute | solution.py:878
  34.3 0.8 copy-start.4
  86.2 3.3 %copy-start.1 = (bf16[3328,128]{1,0:T(8,128)(2,1)S(1)}, bf16[3328,128]{1,0:T(8,128)(2,1)}, u32[]{:S(2)}) copy-start(bf16[3328,128]{1,0:T(8,128)(2,1)} %get-tuple-element.82) | copy-start | bytes 2555908
  86.3 3.3 %collective-permute-start.4 = (bf16[3328,128]{1,0:T(8,128)(2,1)}, bf16[3328,128]{1,0:T(8,128)(2,1)S(1)}, u32[]{:S(2)}, u32[]{:S(2)}) collective-permute-start(bf16[3328,128]{1,0:T(8,128)(2,1)} %get-tuple-element.83), channel_id=1, source_target_pairs={{0,1},{1,0},{2,3},{3,2},{4,5},{5,4},{6,7},{7,6},{8,9},{9,8},{10,11... | collective-permute-start | bytes 2555912 | tf_op jit(solution)/shard_map/ppermute | solution.py:878
  88.6 35.5 %collective-permute-start.5 = (bf16[8,357,128]{2,0,1:T(8,128)(2,1)}, bf16[8,357,128]{2,0,1:T(8,128)(2,1)S(1)}, u32[]{:S(2)}, u32[]{:S(2)}) collective-permute-start(bf16[8,357,128]{2,0,1:T(8,128)(2,1)} %copy.38), channel_id=1, source_target_pairs={{0,16},{16,0},{1,17},{17,1},{2,18},{18,2},{3,19},{19,3},{4,20},{20... | collective-permute-start | bytes 2193416 | tf_op jit(solution)/shard_map/ppermute | solution.py:875
  90.6 33.4 %all-to-all-start = ((bf16[8,416,128]{2,1,0:T(8,128)(2,1)}), bf16[8,416,128]{2,1,0:T(8,128)(2,1)S(1)}, u32[]{:S(2)}, u32[]{:S(2)}) async-start(bf16[8,416,128]{2,1,0:T(8,128)(2,1)} %bitcast.7), calls=%async_computation | async-start | bytes 1703936 | tf_op jit(solution)/shard_map/all_to_all | solution.py:889
  124.1 3.2 %collective-permute-start.6 = (bf16[3328,128]{1,0:T(8,128)(2,1)}, bf16[3328,128]{1,0:T(8,128)(2,1)S(1)}, u32[]{:S(2)}, u32[]{:S(2)}) collective-permute-start(bf16[3328,128]{1,0:T(8,128)(2,1)} %get-tuple-element.104), channel_id=1, source_target_pairs={{0,1},{1,0},{2,3},{3,2},{4,5},{5,4},{6,7},{7,6},{8,9},{9,8},{10,11... | collective-permute-start | bytes 2555912 | tf_op jit(solution)/shard_map/ppermute | solution.py:878
  125.3 7.3 %collective-permute-start.7 = (bf16[2,357,128]{2,0,1:T(2,128)(2,1)S(1)}, bf16[2,357,128]{2,0,1:T(2,128)(2,1)S(1)}, u32[]{:S(2)}, u32[]{:S(2)}) collective-permute-start(bf16[2,357,128]{2,0,1:T(2,128)(2,1)S(1)} %copy.39), channel_id=1, source_target_pairs={{0,16},{16,0},{1,17},{17,1},{2,18},{18,2},{3,19},{19,3},{4,20},{20... | collective-permute-start | bytes 548360 | tf_op jit(solution)/shard_map/ppermute | solution.py:875
  132.5 20.3 %all-to-all-start.1 = ((bf16[8,416,128]{2,1,0:T(8,128)(2,1)}), bf16[8,416,128]{2,1,0:T(8,128)(2,1)S(1)}, u32[]{:S(2)}, u32[]{:S(2)}) async-start(bf16[8,416,128]{2,1,0:T(8,128)(2,1)} %bitcast.8), calls=%async_computation.1 | async-start | bytes 1703936 | tf_op jit(solution)/shard_map/all_to_all | solution.py:889
  137.5 17.1 %collective-permute-start.10 = (bf16[416,128]{1,0:T(8,128)(2,1)S(1)}, bf16[416,128]{1,0:T(8,128)(2,1)S(1)}, u32[]{:S(2)}, u32[]{:S(2)}) collective-permute-start(bf16[416,128]{1,0:T(8,128)(2,1)S(1)} %reduce_sum.25), channel_id=1, source_target_pairs={{0,8},{1,9},{2,10},{3,11},{4,12},{5,13},{6,14},{7,15},{8,0},{9,1},... | collective-permute-start | bytes 319496 | tf_op jit(solution)/shard_map/ppermute | solution.py:892
  140.2 20.6 %collective-permute-start.9 = (bf16[6,357,128]{2,1,0:T(8,128)(2,1)}, bf16[6,357,128]{2,1,0:T(8,128)(2,1)S(1)}, u32[]{:S(2)}, u32[]{:S(2)}) collective-permute-start(bf16[6,357,128]{2,1,0:T(8,128)(2,1)} %get-tuple-element.109), channel_id=1, source_target_pairs={{0,16},{16,0},{1,17},{17,1},{2,18},{18,2},{3,19},{19,3},{4,20},{20... | collective-permute-start | bytes 1645064 | tf_op jit(solution)/shard_map/ppermute | solution.py:875
  153.0 6.2 %collective-permute-start.8 = (bf16[416,128]{1,0:T(8,128)(2,1)S(1)}, bf16[416,128]{1,0:T(8,128)(2,1)S(1)}, u32[]{:S(2)}, u32[]{:S(2)}) collective-permute-start(bf16[416,128]{1,0:T(8,128)(2,1)S(1)} %reduce_sum.24), channel_id=1, source_target_pairs={{0,8},{1,9},{2,10},{3,11},{4,12},{5,13},{6,14},{7,15},{8,0},{9,1},... | collective-permute-start | bytes 319496 | tf_op jit(solution)/shard_map/ppermute | solution.py:892
  161.8 17.1 %all-to-all-start.2 = ((bf16[8,416,128]{2,1,0:T(8,128)(2,1)}), bf16[8,416,128]{2,1,0:T(8,128)(2,1)S(1)}, u32[]{:S(2)}, u32[]{:S(2)}) async-start(bf16[8,416,128]{2,1,0:T(8,128)(2,1)} %pad_maximum_fusion), calls=%async_computation.2 | async-start | bytes 1703936 | tf_op jit(solution)/shard_map/all_to_all | solution.py:889
  179.0 2.4 %copy-start = (bf16[8,416,128]{2,1,0:T(8,128)(2,1)}, bf16[8,416,128]{2,1,0:T(8,128)(2,1)S(1)}, u32[]{:S(2)}) copy-start(bf16[8,416,128]{2,1,0:T(8,128)(2,1)S(1)} %all-to-all-done.2) | copy-start | bytes 2555908
  179.0 2.4 %collective-permute-start.11 = (bf16[8,416,128]{2,1,0:T(8,128)(2,1)S(1)}, bf16[8,416,128]{2,1,0:T(8,128)(2,1)S(1)}, u32[]{:S(2)}, u32[]{:S(2)}) collective-permute-start(bf16[8,416,128]{2,1,0:T(8,128)(2,1)S(1)} %all-to-all-done.2), channel_id=1, source_target_pairs={{0,1},{1,0},{2,3},{3,2},{4,5},{5,4},{6,7},{7,6},{8,9},{9,8},{10,11... | collective-permute-start | bytes 2555912 | tf_op jit(solution)/shard_map/ppermute | solution.py:878
  181.3 1.0 copy-start.2

commit v3 on v1

--- a/solution.py
+++ b/solution.py
@@ -163,19 +163,20 @@
 
     def scores(u):
         p, member = units[u]
-        for t, (at, stop, _) in enumerate(TILES):
-            T.s[u % 3, 0:stop, 256 * t : 256 * t + 256] = dot_upper(
+        for t, (at, stop, sure) in enumerate(TILES):
+            lanes = slice(256 * t, 256 * t + 256)
+            both = dot_upper(
                 T.k[of(member, 0, stop), 128 * p : 128 * p + 128],
                 two_heads(S.q, p, of(member, at, at + 128)),
             )
+            if sure:
+                T.s[u % 3, 0:sure, lanes] = both[0:sure]
+            mask = twice(T.mask[member, t, 0 : stop - sure, :])
+            T.s[u % 3, sure:stop, lanes] = both[sure:stop] + mask
 
     def strips(u, t, side):
-        _, stop, sure = TILES[t]
-        for start in range(0, stop, 16):
-            value = T.s[u % 3, start : start + 16, column_of(t, side)]
-            if start >= sure:
-                value = value + T.mask[units[u][1], t, start - sure : start - sure + 16, :]
-            yield start, value
+        for start in range(0, TILES[t][1], 16):
+            yield start, T.s[u % 3, start : start + 16, column_of(t, side)]
 
     columns = [(t, side) for t in range(3) for side in range(2)]
 
@@ -518,14 +519,14 @@
             emit_half(refs.send, 0, 1 - half, refs)
 
 
-def pack_kernel(place, *refs):
+def pack_kernel(*refs):
     vec, half = refs[-2:]
     inw, outw = refs[8:10]
     at = 0
     for ref in refs[:8]:
         vec[:, at : at + ref.shape[1]] = ref[...]
         at += ref.shape[1]
-    rows = pl.ds(pl.multiple_of(place[2] * 128, 128), 128)
+    rows = pl.ds(pl.multiple_of(lax.axis_index("batch") % 2 * 128, 128), 128)
     half[0:128, 0:768] = inw[0, rows, :]
     half[0:128, 768:1024] = outw[0, rows, :]
     rest = jnp.concatenate([vec[:, 1024 * j : 1024 * j + 1024] for j in range(3)], axis=0)
@@ -538,10 +539,11 @@
     half[128:144, :] = jnp.concatenate(parts, axis=0).astype(bf16)
 
 
-def pack_feed_kernel(place, upw, dnw, half):
-    half[0:128, :] = upw[0, pl.ds(pl.multiple_of(place[2] * 128, 128), 128), :]
+def pack_feed_kernel(upw, dnw, half):
+    core = lax.axis_index("batch") % 2
+    half[0:128, :] = upw[0, pl.ds(pl.multiple_of(core * 128, 128), 128), :]
     for j in range(4):
-        rows = pl.ds(pl.multiple_of(place[2] * 512 + 128 * j, 128), 128)
+        rows = pl.ds(pl.multiple_of(core * 512 + 128 * j, 128), 128)
         half[128:256, 256 * j : 256 * j + 256] = dnw[0, rows, :]
 
 
@@ -568,6 +570,8 @@
         load_padded(refs.x, member, refs.tokens.at[member], length)
         lines.append(refs.frames[pl.ds(place[0] + PAIR * step + member, 1), :])
     forward_attend(refs.x, lines, refs, refs, refs)
+    for _, _, _, rows in chunks():
+        refs.slim[rows, :] = refs.middle[rows, :].astype(bf16)
 
 
 def middle_kernel(place, refs):
@@ -871,14 +875,13 @@
 
     vectors, half_weights = pl.pallas_call(
         pack_kernel,
-        in_specs=[SMEM] + [VMEM] * 10,
+        in_specs=[VMEM] * 10,
         out_specs=[VMEM] * 2,
         out_shape=[
             jax.ShapeDtypeStruct((1, 3072), f32),
             jax.ShapeDtypeStruct((144, 1024), bf16),
         ],
     )(
-        place,
         attend_gain,
         attend_shift,
         inward_bias,
@@ -893,12 +896,12 @@
     own_attend = (vectors, inward_weight[0], outward_weight[0])
     half_feed = pl.pallas_call(
         pack_feed_kernel,
-        in_specs=[SMEM] + [VMEM] * 2,
+        in_specs=[VMEM] * 2,
         out_specs=VMEM,
         out_shape=jax.ShapeDtypeStruct((256, 1024), bf16),
-    )(place, up_weight, down_weight)
-    arrived, half_feed, held_tokens, held_cotangent = lax.optimization_barrier(
-        (across(half_weights), half_feed, mine(tokens), mine(cotangent))
+    )(up_weight, down_weight)
+    arrived, half_feed, held_tokens, held_cotangent, place = lax.optimization_barrier(
+        (across(half_weights), half_feed, mine(tokens), mine(cotangent), place)
     )
     far_attend = (arrived, between_cores(arrived))
     arrived_feed = across(half_feed)
@@ -907,10 +910,10 @@
         return constant((sequences, length)), frame_ids
 
     table = dict(ATTEND_SAVED)
-    table.update(middle=BETWEEN["middle"])
+    table.update(slim=((BOTH, 256), bf16, 0))
     scratch = dict(ATTEND_SCRATCH)
     scratch.update(ATTEND_WEIGHTS)
-    scratch.update(second=BETWEEN["second"])
+    scratch.update(BETWEEN)
     kept = call(
         attend_kernel,
         steps,
@@ -955,7 +958,7 @@
         far,
         dict(
             low_n2=(step_spec((BOTH, 256)), kept["n2"]),
-            low_middle=(step_spec((BOTH, 256)), kept["middle"]),
+            low_middle=(step_spec((BOTH, 256)), kept["slim"]),
             cotangent=(step_spec((PAIR, length, 256)), held_cotangent),
             frames=whole_frames(),
         ),

time: 188 us -> 187 us (level)
  transfers between devices with their start and end apart: 15 -> 15, of which waited for: 8 -> 8; matrix products, arithmetic and copies ran while one was open for 10% -> 11% of each run, Pallas kernels for 25% -> 25%
where the time goes in v3:
time: 187 us; the launch traced here: 186 us
  Pallas kernels  105 us (56%)
  waiting for transfers between devices  29.7 us (16%)
  starting transfers between devices  27 us (14%)
  other arithmetic  13.1 us (7%)
  local copies, waits for them, and re-layouts  10.8 us (6%)
    pallas_call x3, Pallas kernels, call(): pl.pallas_call(run, grid_spec=pltpu.PrefetchScalarGridSpec(num_scalar_pre...  96.3 us
    all_to_all x3, waiting for transfers between devices, exchange(): lax.all_to_all(value, everyone, 0, 0, tiled=True, axis_index_groups=cubes)  16.2 us
    all_to_all x3, starting transfers between devices, exchange(): lax.all_to_all(value, everyone, 0, 0, tiled=True, axis_index_groups=cubes)  12.7 us
    ppermute x5, starting transfers between devices, across(): return lax.ppermute(value, 'section', ((0, 1), (1, 0)))  9.67 us
    select_n x2, other arithmetic, assemble(): value = jnp.where(ours, held.transpose(1, 0, 2), arrived.transpose(1, 0, 2))  7.76 us
    pallas_call x1, Pallas kernels, body(): pl.pallas_call(final_kernel, in_specs=[SMEM] + [VMEM] * 8, out_specs=[VME...  4.67 us
    ppermute x2, waiting for transfers between devices, partner(): return lax.ppermute(value, 'batch', [(b, b ^ flip) for b in range(batches)])  4.6 us
    ppermute x5, waiting for transfers between devices, across(): return lax.ppermute(value, 'section', ((0, 1), (1, 0)))  4.51 us
  transfers between devices with their start and end apart: 15, of which 8 were waited for; matrix products, arithmetic and copies ran while one was open for 11% of the time, Pallas kernels for 25%

profile of v3, /device:TPU:0, one launch (start us, length us, event | category | flops | bytes accessed | tf_op | source)
XLA Modules:
  0.0 186.4 jit_solution(18424699682041989927)
XLA Ops:
  0.6 1.9 %shard_map.254 = (f32[1,3072]{1,0:T(1,128)}, bf16[144,1024]{1,0:T(8,128)(2,1)}) custom-call(f32[1,256]{1,0:T(1,128)} %refs_2_.3, f32[1,256]{1,0:T(1,128)} %refs_3_.3, f32[1,512]{1,0:T(1,128)} %refs_2_.2, f32[1,256]{1,0:T(1,128)} %refs_3_.2, f32[1,256]{1,0:T(1,128)} %refs_4_.3, f32[1,256]{1,0:T(1,128)} %refs_5_.3, f32[1,1024]{1,0:T(1,128)} %refs_6_.2, ...), custom_call_target="tpu_custom_call" | custom-call | tf_op jit(solution)/shard_map/pallas_call | solution.py:876
  2.6 2.9 %collective-permute-start = (bf16[144,1024]{1,0:T(8,128)(2,1)}, bf16[144,1024]{1,0:T(8,128)(2,1)S(1)}, u32[]{:S(2)}, u32[]{:S(2)}) collective-permute-start(bf16[144,1024]{1,0:T(8,128)(2,1)} %get-tuple-element.73), channel_id=1, source_target_pairs={{0,16},{16,0},{1,17},{17,1},{2,18},{18,2},{3,19},{19,3},{4,20},{20... | collective-permute-start | bytes 884744 | tf_op jit(solution)/shard_map/ppermute | solution.py:857
  5.5 2.0 %constant_dynamic-slice_fusion = (bf16[8,357,256]{2,0,1:T(8,128)(2,1)S(1)}, bf16[8,357,256]{2,0,1:T(8,128)(2,1)S(1)}) fusion(bf16[16,357,256]{2,0,1:T(8,128)(2,1)} %param.16, s32[]{:T(128)S(6)} %select_n.34, bf16[16,357,256]{2,0,1:T(8,128)(2,1)} %param.15), kind=kLoop, calls=%fused_computation.15 | loop fusion | bytes 5849092 | tf_op jit(solution)/shard_map/dynamic_slice | solution.py:854
  7.5 1.4 copy.45.refs_11_
  8.9 1.4 copy.44.refs_5_
  10.4 2.0 %shard_map.255 = bf16[256,1024]{1,0:T(8,128)(2,1)} custom-call(bf16[1,256,1024]{2,1,0:T(8,128)(2,1)} %refs_1_.3, bf16[1,1024,256]{2,1,0:T(8,128)(2,1)} %dnw.1), custom_call_target="tpu_custom_call" | custom-call | tf_op jit(solution)/shard_map/pallas_call | solution.py:897
  12.4 0.7 pad_add_fusion.place
  13.1 0.0 collective-permute-done.refs_3_.refs_5_
  13.1 1.4 collective-permute-start.2
  14.5 0.2 collective-permute-done.1.refs_4_.refs_6_
  14.7 0.7 copy-done.6
  15.4 16.4 %shard_map.256 = (bf16[3072,256]{1,0:T(8,128)(2,1)}, bf16[3072,128]{1,0:T(8,128)(2,1)}, bf16[3072,256]{1,0:T(8,128)(2,1)}, bf16[256,3072]{1,0:T(8,128)(2,1)}, bf...) custom-call(s32[3]{0:T(128)} %pad_add_fusion.place, ...), custom_call_target="tpu_custom_call" | custom-call | flops 17999998976 | bytes 3000000 | tf_op jit(solution)/shard_map/pallas_call | solution.py:809
  31.8 0.2 collective-permute-start.3
  32.0 1.8 collective-permute-done.3.refs_8_
  33.8 0.8 copy-done.4
  34.6 51.1 %shard_map.257 = (bf16[3072,1024]{1,0:T(8,128)(2,1)}, bf16[3072,1024]{1,0:T(8,128)(2,1)}, bf16[3072,256]{1,0:T(8,128)(2,1)}, bf16[16,357,128]{2,1,0:T(8,128)(2,1...) custom-call(s32[3]{0:T(128)} %pad_add_fusion.place, ...), custom_call_target="tpu_custom_call" | custom-call | flops 71999995904 | bytes 3000000 | tf_op jit(solution)/shard_map/pallas_call | solution.py:809
  85.7 0.0 copy-start.1
  85.7 0.2 collective-permute-start.4
  85.9 2.1 %copy.38 = bf16[8,357,128]{2,0,1:T(8,128)(2,1)} copy(bf16[8,357,128]{2,1,0:T(8,128)(2,1)} %get-tuple-element.88) | data formatting | bytes 1462272 | tf_op jit(solution)/shard_map/pallas_call | solution.py:809
  88.0 1.3 collective-permute-start.5
  89.3 1.1 add_convert_fusion.1
  90.5 4.2 %all-to-all-start = ((bf16[8,416,128]{2,1,0:T(8,128)(2,1)}), bf16[8,416,128]{2,1,0:T(8,128)(2,1)S(1)}, u32[]{:S(2)}, u32[]{:S(2)}) async-start(bf16[8,416,128]{2,1,0:T(8,128)(2,1)} %bitcast.7), calls=%async_computation | async-start | bytes 1703936 | tf_op jit(solution)/shard_map/all_to_all | solution.py:871
  94.7 28.8 %shard_map.258 = (f32[16,357,128]{2,1,0:T(8,128)}, bf16[6,357,128]{2,1,0:T(8,128)(2,1)}, bf16[2,357,128]{2,1,0:T(8,128)(2,1)}, bf16[3328,128]{1,0:T(8,128)(2,1)}, bf16[3328,128]{1,0:T(8,128)(2,1)}) custom-call(s32[3]{0:T(128)} %pad_add_fusion.place, f32[1,3072]{1,0:T(1,128)} %get-tuple-element.75.refs_0_, bf16[256,768]{1,0:T(8,128)(2,1)} %bitcast.23, ...), custom_call_target="tpu_custom_call" | custom-call | flops 40000000000 | bytes 3000000 | tf_op jit(solution)/shard_map/pallas_call | solution.py:809
  123.5 0.1 collective-permute-start.6
  123.6 1.1 copy.39
  124.7 2.0 %collective-permute-start.7 = (bf16[2,357,128]{2,0,1:T(2,128)(2,1)S(1)}, bf16[2,357,128]{2,0,1:T(2,128)(2,1)S(1)}, u32[]{:S(2)}, u32[]{:S(2)}) collective-permute-start(bf16[2,357,128]{2,0,1:T(2,128)(2,1)S(1)} %copy.39), channel_id=1, source_target_pairs={{0,16},{16,0},{1,17},{17,1},{2,18},{18,2},{3,19},{19,3},{4,20},{20... | collective-permute-start | bytes 548360 | tf_op jit(solution)/shard_map/ppermute | solution.py:857
  126.7 2.3 %add_convert_fusion = bf16[3328,128]{1,0:T(8,128)(2,1)} fusion(bf16[3328,128]{1,0:T(8,128)(2,1)S(1)} %collective-permute-done.6, bf16[3328,128]{1,0:T(8,128)(2,1)} %get-tuple-element.105), kind=kLoop, calls=%fused_computation.2 | loop fusion | flops 1703936 | bytes 2555904 | tf_op jit(solution)/shard_map/convert_element_type | solution.py:976
  129.0 3.0 %collective-permute-done.7 = bf16[2,357,128]{2,0,1:T(2,128)(2,1)S(1)} collective-permute-done((bf16[2,357,128]{2,0,1:T(2,128)(2,1)S(1)}, bf16[2,357,128]{2,0,1:T(2,128)(2,1)S(1)}, u32[]{:S(2)}, u32[]{:S(2)}) %collective-permute-start.7) | collective-permute-done | bytes 182816 | tf_op jit(solution)/shard_map/ppermute | solution.py:857
  132.0 4.8 %all-to-all-start.1 = ((bf16[8,416,128]{2,1,0:T(8,128)(2,1)}), bf16[8,416,128]{2,1,0:T(8,128)(2,1)S(1)}, u32[]{:S(2)}, u32[]{:S(2)}) async-start(bf16[8,416,128]{2,1,0:T(8,128)(2,1)} %bitcast.8), calls=%async_computation.1 | async-start | bytes 1703936 | tf_op jit(solution)/shard_map/all_to_all | solution.py:871
  136.8 0.1 reduce_sum.25
  136.9 2.6 %collective-permute-start.10 = (bf16[416,128]{1,0:T(8,128)(2,1)S(1)}, bf16[416,128]{1,0:T(8,128)(2,1)S(1)}, u32[]{:S(2)}, u32[]{:S(2)}) collective-permute-start(bf16[416,128]{1,0:T(8,128)(2,1)S(1)} %reduce_sum.25), channel_id=1, source_target_pairs={{0,8},{1,9},{2,10},{3,11},{4,12},{5,13},{6,14},{7,15},{8,0},{9,1},... | collective-permute-start | bytes 319496 | tf_op jit(solution)/shard_map/ppermute | solution.py:874
  139.6 2.0 %collective-permute-start.9 = (bf16[6,357,128]{2,1,0:T(8,128)(2,1)}, bf16[6,357,128]{2,1,0:T(8,128)(2,1)S(1)}, u32[]{:S(2)}, u32[]{:S(2)}) collective-permute-start(bf16[6,357,128]{2,1,0:T(8,128)(2,1)} %get-tuple-element.111), channel_id=1, source_target_pairs={{0,16},{16,0},{1,17},{17,1},{2,18},{18,2},{3,19},{19,3},{4,20},{20... | collective-permute-start | bytes 1645064 | tf_op jit(solution)/shard_map/ppermute | solution.py:857
  141.6 3.1 %fusion.1 = bf16[357,16,128]{2,1,0:T(8,128)(2,1)} fusion(bf16[8,357,128]{2,0,1:T(8,128)(2,1)S(1)} %collective-permute-done.5, bf16[16,357,128]{2,1,0:T(8,128)(2,1)} %get-tuple-element.109, pred[16]{0:T(512)(128)(4,1)S(1)} %fusion.2), kind=kLoop, calls=%fused_computation.5 | loop fusion | flops 3655680 | bytes 3655696 | tf_op jit(solution)/shard_map/jit(_where)/select_n | solution.py:1055
  144.7 7.6 %all-to-all-done.1 = bf16[8,416,128]{2,1,0:T(8,128)(2,1)S(1)} async-done(((bf16[8,416,128]{2,1,0:T(8,128)(2,1)}), bf16[8,416,128]{2,1,0:T(8,128)(2,1)S(1)}, u32[]{:S(2)}, u32[]{:S(2)}) %all-to-all-start.1) | async-done | bytes 852000 | tf_op jit(solution)/shard_map/all_to_all | solution.py:871
  152.3 0.1 reduce_sum.24
  152.4 1.5 collective-permute-start.8
  154.0 4.6 %collective-permute-done.8 = bf16[416,128]{1,0:T(8,128)(2,1)S(1)} collective-permute-done((bf16[416,128]{1,0:T(8,128)(2,1)S(1)}, bf16[416,128]{1,0:T(8,128)(2,1)S(1)}, u32[]{:S(2)}, u32[]{:S(2)}) %collective-permute-start.8) | collective-permute-done | bytes 106528 | tf_op jit(solution)/shard_map/ppermute | solution.py:874
  158.6 1.5 collective-permute-done.9
  160.1 0.1 broadcast_in_dim.23
  160.2 0.1 broadcast_in_dim.22
  160.3 1.0 pad_maximum_fusion
  161.2 3.7 %all-to-all-start.2 = ((bf16[8,416,128]{2,1,0:T(8,128)(2,1)}), bf16[8,416,128]{2,1,0:T(8,128)(2,1)S(1)}, u32[]{:S(2)}, u32[]{:S(2)}) async-start(bf16[8,416,128]{2,1,0:T(8,128)(2,1)} %pad_maximum_fusion), calls=%async_computation.2 | async-start | bytes 1703936 | tf_op jit(solution)/shard_map/all_to_all | solution.py:871
  165.0 0.1 copy.41
  165.1 4.7 %fusion = f32[357,16,128]{2,1,0:T(8,128)} fusion(f32[16,357,128]{2,1,0:T(8,128)} %get-tuple-element.115, bf16[2,357,128]{2,0,1:T(2,128)(2,1)S(1)} %collective-permute-done.7, bf16[6,357,128]{2,0,1:T(8,128)(2,1)S(1)} %copy.41, pred[16]{0:T(512)(128)(4,1)S(1)} %fusion.2), kind=kLoop, calls=%fused_computation.1 | loop fusion | flops 6580224 | bytes 6580240 | tf_op jit(solution)/shard_map/jit(_where)/select_n | solution.py:1055
  169.8 8.6 %all-to-all-done.2 = bf16[8,416,128]{2,1,0:T(8,128)(2,1)S(1)} async-done(((bf16[8,416,128]{2,1,0:T(8,128)(2,1)}), bf16[8,416,128]{2,1,0:T(8,128)(2,1)S(1)}, u32[]{:S(2)}, u32[]{:S(2)}) %all-to-all-start.2) | async-done | bytes 852000 | tf_op jit(solution)/shard_map/all_to_all | solution.py:871
  178.4 2.4 %collective-permute-done.11 = bf16[8,416,128]{2,1,0:T(8,128)(2,1)S(1)} collective-permute-done((bf16[8,416,128]{2,1,0:T(8,128)(2,1)S(1)}, bf16[8,416,128]{2,1,0:T(8,128)(2,1)S(1)}, u32[]{:S(2)}, u32[]{:S(2)}) %collective-permute-start.11) | collective-permute-done | bytes 852000 | tf_op jit(solution)/shard_map/ppermute | solution.py:860
  180.8 0.9 copy-done.2
  181.7 4.7 %shard_map.259 = (f32[1,256]{1,0:T(1,128)}, f32[1,256]{1,0:T(1,128)}, f32[1,256,768]{2,1,0:T(8,128)}, f32[1,512]{1,0:T(1,128)}, f32[1,256,256]{2,1,0:T(8,128)}, ...) custom-call(s32[3]{0:T(128)} %pad_add_fusion.place, ...), custom_call_target="tpu_custom_call" | custom-call | tf_op jit(solution)/shard_map/pallas_call | solution.py:1086
  (21 shorter events, 0.1 us)
Async XLA Ops:
  2.6 10.5 %collective-permute-start = (bf16[144,1024]{1,0:T(8,128)(2,1)}, bf16[144,1024]{1,0:T(8,128)(2,1)S(1)}, u32[]{:S(2)}, u32[]{:S(2)}) collective-permute-start(bf16[144,1024]{1,0:T(8,128)(2,1)} %get-tuple-element.73), channel_id=1, source_target_pairs={{0,16},{16,0},{1,17},{17,1},{2,18},{18,2},{3,19},{19,3},{4,20},{20... | collective-permute-start | bytes 884744 | tf_op jit(solution)/shard_map/ppermute | solution.py:857
  13.1 1.6 copy-start.5
  13.1 1.6 collective-permute-start.1
  13.1 18.7 %collective-permute-start.2 = (bf16[256,1024]{1,0:T(8,128)(2,1)}, bf16[256,1024]{1,0:T(8,128)(2,1)S(1)}, u32[]{:S(2)}, u32[]{:S(2)}) collective-permute-start(bf16[256,1024]{1,0:T(8,128)(2,1)} %shard_map.255), channel_id=1, source_target_pairs={{0,16},{16,0},{1,17},{17,1},{2,18},{18,2},{3,19},{19,3},{4,20},{20... | collective-permute-start | bytes 1572872 | tf_op jit(solution)/shard_map/ppermute | solution.py:857
  14.7 0.7 copy-start.6
  31.8 2.0 %copy-start.3 = (bf16[256,1024]{1,0:T(8,128)(2,1)}, bf16[256,1024]{1,0:T(8,128)(2,1)S(1)}, u32[]{:S(2)}) copy-start(bf16[256,1024]{1,0:T(8,128)(2,1)S(1)} %collective-permute-done.2.refs_7_) | copy-start | bytes 1572868
  31.8 2.0 %collective-permute-start.3 = (bf16[256,1024]{1,0:T(8,128)(2,1)S(1)}, bf16[256,1024]{1,0:T(8,128)(2,1)S(1)}, u32[]{:S(2)}, u32[]{:S(2)}) collective-permute-start(bf16[256,1024]{1,0:T(8,128)(2,1)S(1)} %collective-permute-done.2.refs_7_), channel_id=1, source_target_pairs={{0,1},{1,0},{2,3},{3,2},{4,5},{5,4},{6,7},{7,6},{8,9},{9,8},{10,11... | collective-permute-start | bytes 1572872 | tf_op jit(solution)/shard_map/ppermute | solution.py:860
  33.8 0.8 copy-start.4
  85.7 3.6 %copy-start.1 = (bf16[3328,128]{1,0:T(8,128)(2,1)S(1)}, bf16[3328,128]{1,0:T(8,128)(2,1)}, u32[]{:S(2)}) copy-start(bf16[3328,128]{1,0:T(8,128)(2,1)} %get-tuple-element.84) | copy-start | bytes 2555908
  85.7 3.6 %collective-permute-start.4 = (bf16[3328,128]{1,0:T(8,128)(2,1)}, bf16[3328,128]{1,0:T(8,128)(2,1)S(1)}, u32[]{:S(2)}, u32[]{:S(2)}) collective-permute-start(bf16[3328,128]{1,0:T(8,128)(2,1)} %get-tuple-element.85), channel_id=1, source_target_pairs={{0,1},{1,0},{2,3},{3,2},{4,5},{5,4},{6,7},{7,6},{8,9},{9,8},{10,11... | collective-permute-start | bytes 2555912 | tf_op jit(solution)/shard_map/ppermute | solution.py:860
  88.0 35.5 %collective-permute-start.5 = (bf16[8,357,128]{2,0,1:T(8,128)(2,1)}, bf16[8,357,128]{2,0,1:T(8,128)(2,1)S(1)}, u32[]{:S(2)}, u32[]{:S(2)}) collective-permute-start(bf16[8,357,128]{2,0,1:T(8,128)(2,1)} %copy.38), channel_id=1, source_target_pairs={{0,16},{16,0},{1,17},{17,1},{2,18},{18,2},{3,19},{19,3},{4,20},{20... | collective-permute-start | bytes 2193416 | tf_op jit(solution)/shard_map/ppermute | solution.py:857
  90.5 33.0 %all-to-all-start = ((bf16[8,416,128]{2,1,0:T(8,128)(2,1)}), bf16[8,416,128]{2,1,0:T(8,128)(2,1)S(1)}, u32[]{:S(2)}, u32[]{:S(2)}) async-start(bf16[8,416,128]{2,1,0:T(8,128)(2,1)} %bitcast.7), calls=%async_computation | async-start | bytes 1703936 | tf_op jit(solution)/shard_map/all_to_all | solution.py:871
  123.5 3.2 %collective-permute-start.6 = (bf16[3328,128]{1,0:T(8,128)(2,1)}, bf16[3328,128]{1,0:T(8,128)(2,1)S(1)}, u32[]{:S(2)}, u32[]{:S(2)}) collective-permute-start(bf16[3328,128]{1,0:T(8,128)(2,1)} %get-tuple-element.106), channel_id=1, source_target_pairs={{0,1},{1,0},{2,3},{3,2},{4,5},{5,4},{6,7},{7,6},{8,9},{9,8},{10,11... | collective-permute-start | bytes 2555912 | tf_op jit(solution)/shard_map/ppermute | solution.py:860
  124.7 7.3 %collective-permute-start.7 = (bf16[2,357,128]{2,0,1:T(2,128)(2,1)S(1)}, bf16[2,357,128]{2,0,1:T(2,128)(2,1)S(1)}, u32[]{:S(2)}, u32[]{:S(2)}) collective-permute-start(bf16[2,357,128]{2,0,1:T(2,128)(2,1)S(1)} %copy.39), channel_id=1, source_target_pairs={{0,16},{16,0},{1,17},{17,1},{2,18},{18,2},{3,19},{19,3},{4,20},{20... | collective-permute-start | bytes 548360 | tf_op jit(solution)/shard_map/ppermute | solution.py:857
  132.0 20.3 %all-to-all-start.1 = ((bf16[8,416,128]{2,1,0:T(8,128)(2,1)}), bf16[8,416,128]{2,1,0:T(8,128)(2,1)S(1)}, u32[]{:S(2)}, u32[]{:S(2)}) async-start(bf16[8,416,128]{2,1,0:T(8,128)(2,1)} %bitcast.8), calls=%async_computation.1 | async-start | bytes 1703936 | tf_op jit(solution)/shard_map/all_to_all | solution.py:871
  136.9 17.0 %collective-permute-start.10 = (bf16[416,128]{1,0:T(8,128)(2,1)S(1)}, bf16[416,128]{1,0:T(8,128)(2,1)S(1)}, u32[]{:S(2)}, u32[]{:S(2)}) collective-permute-start(bf16[416,128]{1,0:T(8,128)(2,1)S(1)} %reduce_sum.25), channel_id=1, source_target_pairs={{0,8},{1,9},{2,10},{3,11},{4,12},{5,13},{6,14},{7,15},{8,0},{9,1},... | collective-permute-start | bytes 319496 | tf_op jit(solution)/shard_map/ppermute | solution.py:874
  139.6 20.6 %collective-permute-start.9 = (bf16[6,357,128]{2,1,0:T(8,128)(2,1)}, bf16[6,357,128]{2,1,0:T(8,128)(2,1)S(1)}, u32[]{:S(2)}, u32[]{:S(2)}) collective-permute-start(bf16[6,357,128]{2,1,0:T(8,128)(2,1)} %get-tuple-element.111), channel_id=1, source_target_pairs={{0,16},{16,0},{1,17},{17,1},{2,18},{18,2},{3,19},{19,3},{4,20},{20... | collective-permute-start | bytes 1645064 | tf_op jit(solution)/shard_map/ppermute | solution.py:857
  152.4 6.2 %collective-permute-start.8 = (bf16[416,128]{1,0:T(8,128)(2,1)S(1)}, bf16[416,128]{1,0:T(8,128)(2,1)S(1)}, u32[]{:S(2)}, u32[]{:S(2)}) collective-permute-start(bf16[416,128]{1,0:T(8,128)(2,1)S(1)} %reduce_sum.24), channel_id=1, source_target_pairs={{0,8},{1,9},{2,10},{3,11},{4,12},{5,13},{6,14},{7,15},{8,0},{9,1},... | collective-permute-start | bytes 319496 | tf_op jit(solution)/shard_map/ppermute | solution.py:874
  161.2 17.1 %all-to-all-start.2 = ((bf16[8,416,128]{2,1,0:T(8,128)(2,1)}), bf16[8,416,128]{2,1,0:T(8,128)(2,1)S(1)}, u32[]{:S(2)}, u32[]{:S(2)}) async-start(bf16[8,416,128]{2,1,0:T(8,128)(2,1)} %pad_maximum_fusion), calls=%async_computation.2 | async-start | bytes 1703936 | tf_op jit(solution)/shard_map/all_to_all | solution.py:871
  178.4 2.4 %copy-start = (bf16[8,416,128]{2,1,0:T(8,128)(2,1)}, bf16[8,416,128]{2,1,0:T(8,128)(2,1)S(1)}, u32[]{:S(2)}) copy-start(bf16[8,416,128]{2,1,0:T(8,128)(2,1)S(1)} %all-to-all-done.2) | copy-start | bytes 2555908
  178.4 2.4 %collective-permute-start.11 = (bf16[8,416,128]{2,1,0:T(8,128)(2,1)S(1)}, bf16[8,416,128]{2,1,0:T(8,128)(2,1)S(1)}, u32[]{:S(2)}, u32[]{:S(2)}) collective-permute-start(bf16[8,416,128]{2,1,0:T(8,128)(2,1)S(1)} %all-to-all-done.2), channel_id=1, source_target_pairs={{0,1},{1,0},{2,3},{3,2},{4,5},{5,4},{6,7},{7,6},{8,9},{9,8},{10,11... | collective-permute-start | bytes 2555912 | tf_op jit(solution)/shard_map/ppermute | solution.py:860
  180.8 0.9 copy-start.2
